TPU v7x, 32 devices: a whole 2x2x4 slice. The times are simulated.
32 devices in a mesh: groups: 2 (over x), dp: 16 (over z, y, core).
Axes of the slice: x: 2, y: 2, z: 4, core: 2. Of those that a mesh axis runs over, the one named last changes fastest.
Arguments:
- train_inputs: bfloat16 [4096, 28672], P('groups', 'dp'), parts along dimension 0, may hold values from -6 to 6
- train_grads: bfloat16 [4096, 8192], P('groups', 'dp'), parts along dimension 0, may hold values from -6 to 6
- query_inputs: bfloat16 [1024, 28672], P('groups', 'dp'), parts along dimension 0, may hold values from -6 to 6
- query_grads: bfloat16 [1024, 8192], P('groups', 'dp'), parts along dimension 0, may hold values from -6 to 6
- proj_in: bfloat16 [64, 28672], P(None, 'dp'), may hold values from -0.03125 to 0.03125
- proj_out: bfloat16 [64, 8192], P(None, 'dp'), may hold values from -0.0625 to 0.0625
Outputs:
- scores: float32 [32, 4], P(('groups', 'dp')), parts along dimension 0
There are 2 independent parts, one for each index of `groups`. A program takes and returns all parts, laid end to end along the dimension named above; an argument that names none is the same for every part. Nothing has to cross between parts.
All inputs are finite; a program needn't handle non-finite values.
Results may differ from a plain program's by a relative error of at most 0.0057.
Values may be sent and summed in bfloat16 or wider, within the bound.
No kernel may reach another device: no remote copies, remote signals or barrier semaphores. Data moves between devices by JAX's collectives and lax.ppermute only.
A program may use at most 128 MiB of HBM per device.

v0:
```python
import jax
import jax.numpy as jnp
from jax import lax
from jax.sharding import PartitionSpec as P

SEQ = 128


def partial_proj(inputs, grads, proj_in, proj_out):
    dims = (((1,), (1,)), ((), ()))
    side_a = lax.dot_general(grads, proj_out, dims, preferred_element_type=jnp.float32)
    side_b = lax.dot_general(inputs, proj_in, dims, preferred_element_type=jnp.float32)
    return jnp.concatenate([side_a, side_b], axis=1)


def outer_sums(projected, count, rank):
    view = projected.reshape(count, -1, 2 * rank)
    return jnp.einsum(
        "nti,ntj->nij", view[:, :, :rank], view[:, :, rank:], preferred_element_type=jnp.float32
    )


def body(train_inputs, train_grads, query_inputs, query_grads, proj_in, proj_out):
    rank = proj_in.shape[0]
    own_inputs, own_grads = (
        lax.all_to_all(train_inputs, "dp", split_axis=0, concat_axis=1, tiled=True),
        lax.all_to_all(train_grads, "dp", split_axis=0, concat_axis=1, tiled=True),
    )
    whole_in, whole_out = (
        lax.all_gather(proj_in, "dp", axis=1, tiled=True),
        lax.all_gather(proj_out, "dp", axis=1, tiled=True),
    )
    projected = partial_proj(own_inputs, own_grads, whole_in, whole_out).astype(jnp.bfloat16)
    train_grad = outer_sums(projected, projected.shape[0] // SEQ, rank)
    query_count = query_inputs.shape[0] // SEQ
    query_proj = lax.psum_scatter(
        partial_proj(query_inputs, query_grads, proj_in, proj_out),
        "dp",
        scatter_dimension=0,
        tiled=True,
    ).astype(jnp.bfloat16)
    piece = outer_sums(query_proj, 1, rank)
    pieces = lax.all_gather(piece, "dp", axis=0, tiled=True)
    query_grad = jnp.sum(pieces.reshape(query_count, -1, rank, rank), axis=1)
    dims = (((1,), (1,)), ((), ()))
    scores = lax.dot_general(
        train_grad.reshape(train_grad.shape[0], rank * rank),
        query_grad.reshape(query_count, rank * rank),
        dims,
        precision=lax.Precision.HIGHEST,
    )
    return scores / (SEQ * rank)


def solution(mesh):
    return jax.shard_map(
        body,
        mesh=mesh,
        in_specs=(
            P("groups", "dp"),
            P("groups", "dp"),
            P("groups", "dp"),
            P("groups", "dp"),
            P(None, "dp"),
            P(None, "dp"),
        ),
        out_specs=P(("groups", "dp"), None),
        check_vma=False,
    )
```

profile of v0, /device:TPU:0, one launch (start us, length us, event | category | flops | bytes accessed | tf_op | source)
XLA Modules:
  0.0 313.2 jit_solution(12958994193992591382)
XLA Ops:
  6.5 0.0 copy-start
  6.5 54.9 %all_to_all.38 = bf16[16,128,512]{2,1,0:T(8,128)(2,1)} all-to-all(bf16[16,128,512]{2,1,0:T(8,128)(2,1)} %bitcast.42), channel_id=1, replica_groups=mesh['groups'=2,'dp'=16] {'dp'}, dimensions={0} | all-to-all | bytes 4194304 | tf_op jit(solution)/shard_map/all_to_all | solution.py:27
  61.5 0.0 copy-start.2
  61.5 0.0 copy-start.3
  61.5 0.0 copy-start.1
  61.5 5.3 %all-to-all-start.1 = ((bf16[16,128,1792]{2,1,0:T(8,128)(2,1)}), bf16[16,128,1792]{2,1,0:T(8,128)(2,1)}, u32[]{:S(2)}, u32[]{:S(2)}) async-start(bf16[16,128,1792]{2,1,0:T(8,128)(2,1)} %bitcast.41), calls=%async_computation.1 | async-start | bytes 14680064 | tf_op jit(solution)/shard_map/all_to_all | solution.py:26
  66.8 0.0 reduce-scatter.4.cloned.1.call-start
  66.8 0.0 copy-done.2
  66.8 0.0 copy-done.3
  66.8 0.3 fusion.5
  67.1 0.0 copy-done
  67.1 0.0 copy-done.1
  67.1 0.7 fusion.6
  67.8 0.8 copy.13
  68.7 0.0 reduce-scatter.4.cloned.1.call-update
  68.7 0.0 all-gather.6.cloned.1.call-start
  68.7 0.7 all-gather.6.cloned.1.call-update
  69.4 0.0 all-gather.4.cloned.1.call-start
  69.5 0.7 all-gather.4.cloned.1.call-update
  70.2 127.1 %reduce-scatter.4.cloned.1.call-done = f32[32,128]{1,0:T(8,128)} async-done(((f32[512,128]{1,0:T(8,128)}), f32[32,128]{1,0:T(8,128)}) %reduce-scatter.4.cloned.1.call-update) | async-done | bytes 16400
  197.3 0.8 copy.14
  198.1 0.1 fusion.4
  198.3 30.6 %all-gather = f32[1024,64]{1,0:T(8,128)S(1)} all-gather(f32[64,64]{1,0:T(8,128)S(1)} %fusion.4), channel_id=2, replica_groups=mesh['groups'=2,'dp'=16] {'dp'}, dimensions={0}, use_global_device_ids=true | all-gather | bytes 278528 | tf_op jit(solution)/shard_map/all_gather | solution.py:43
  228.9 3.9 %copy.9 = bf16[128,16,512]{0,2,1:T(8,128)(2,1)} copy(bf16[128,16,512]{2,0,1:T(8,128)(2,1)} %bitcast.39) | data formatting | bytes 4194304 | tf_op jit(solution)/shard_map/all_to_all | solution.py:27
  232.8 0.0 all-to-all-done.1
  232.8 10.0 %copy.10 = bf16[128,16,1792]{0,2,1:T(8,128)(2,1)} copy(bf16[128,16,1792]{2,0,1:T(8,128)(2,1)} %bitcast.4) | data formatting | bytes 14680064 | tf_op jit(solution)/shard_map/all_to_all | solution.py:26
  242.8 22.3 %all-gather.6.cloned.1.call-done = bf16[64,28672]{1,0:T(8,128)(2,1)} async-done(((bf16[64,1792]{1,0:T(8,128)(2,1)}), bf16[64,28672]{1,0:T(8,128)(2,1)}) %all-gather.6.cloned.1.call-update) | async-done | bytes 3670032 | tf_op jit(solution)/shard_map/all_gather | solution.py:30
  265.1 5.6 %convolution_convert_fusion = bf16[128,64]{0,1:T(8,128)(2,1)S(1)} fusion(bf16[64,28672]{1,0:T(8,128)(2,1)} %all-gather.6.cloned.1.call-done, bf16[128,28672]{0,1:T(8,128)(2,1)} %bitcast.38), kind=kOutput, calls=%fused_computation | convolution fusion | flops 469770240 | bytes 11026432 | tf_op jit(solution)/shard_map/dot_general | solution.py:12
  270.7 32.3 %all-gather.4.cloned.1.call-done = bf16[64,8192]{1,0:T(8,128)(2,1)} async-done(((bf16[64,512]{1,0:T(8,128)(2,1)}), bf16[64,8192]{1,0:T(8,128)(2,1)}) %all-gather.4.cloned.1.call-update) | async-done | bytes 1048592 | tf_op jit(solution)/shard_map/all_gather | solution.py:31
  303.0 2.5 fusion
  305.5 1.2 fusion.2
  (2 shorter events, 0.1 us)
Async XLA Ops:
  6.5 60.6 %copy-start = (bf16[512,1792]{1,0:T(8,128)(2,1)S(1)}, bf16[512,1792]{1,0:T(8,128)(2,1)}, u32[]{:S(2)}) copy-start(bf16[512,1792]{1,0:T(8,128)(2,1)} %param.8) | copy-start | bytes 5505028
  61.5 5.3 %copy-start.2 = (bf16[512,512]{1,0:T(8,128)(2,1)S(1)}, bf16[512,512]{1,0:T(8,128)(2,1)}, u32[]{:S(2)}) copy-start(bf16[512,512]{1,0:T(8,128)(2,1)} %param.9) | copy-start | bytes 1572868
  61.5 5.4 %copy-start.3 = (bf16[64,512]{1,0:T(8,128)(2,1)S(1)}, bf16[64,512]{1,0:T(8,128)(2,1)}, u32[]{:S(2)}) copy-start(bf16[64,512]{1,0:T(8,128)(2,1)} %param.11) | copy-start | bytes 196612
  61.5 5.7 %copy-start.1 = (bf16[64,1792]{1,0:T(8,128)(2,1)S(1)}, bf16[64,1792]{1,0:T(8,128)(2,1)}, u32[]{:S(2)}) copy-start(bf16[64,1792]{1,0:T(8,128)(2,1)} %param.10) | copy-start | bytes 688132
  61.5 171.3 %all-to-all-start.1 = ((bf16[16,128,1792]{2,1,0:T(8,128)(2,1)}), bf16[16,128,1792]{2,1,0:T(8,128)(2,1)}, u32[]{:S(2)}, u32[]{:S(2)}) async-start(bf16[16,128,1792]{2,1,0:T(8,128)(2,1)} %bitcast.41), calls=%async_computation.1 | async-start | bytes 14680064 | tf_op jit(solution)/shard_map/all_to_all | solution.py:26
  66.8 130.5 %reduce-scatter.4.cloned.1.call-start = ((), (), s32[]{:S(2)}) async-start(), calls=%async_computation.5 | async-start | bytes 278528
  68.7 196.4 %all-gather.6.cloned.1.call-start = ((), (), s32[]{:S(2)}) async-start(), calls=%async_computation.4 | async-start | bytes 3899392 | tf_op jit(solution)/shard_map/all_gather | solution.py:30
  69.4 233.5 %all-gather.4.cloned.1.call-start = ((), (), s32[]{:S(2)}) async-start(), calls=%async_computation.3 | async-start | bytes 1114112 | tf_op jit(solution)/shard_map/all_gather | solution.py:31
Sparse Core Ops, SparseCore 0:
  71.1 126.1 reduce-scatter.3
  199.5 65.5 all-gather.5
  267.3 35.6 all-gather.3
where the time goes:
time: 314 us; the launch traced here: 313 us
  waiting for transfers between devices  183 us (58%)
  blocking collectives  85.5 us (27%)
  local copies, waits for them, and re-layouts  15.6 us (5%)
  between operations  13.2 us (4%)
  matrix products  10.4 us (3%)
  starting transfers between devices  5.4 us (2%)
    unnamed x4, waiting for transfers between devices  129 us
    all_to_all x1, blocking collectives, body(): lax.all_to_all(train_grads, 'dp', split_axis=0, concat_axis=1, tiled=True)  54.9 us
    all_gather x1, waiting for transfers between devices, body(): lax.all_gather(proj_out, 'dp', axis=1, tiled=True)  32.3 us
    all_gather x1, blocking collectives, body(): pieces = lax.all_gather(piece, 'dp', axis=0, tiled=True)  30.6 us
    all_gather x1, waiting for transfers between devices, body(): lax.all_gather(proj_in, 'dp', axis=1, tiled=True)  22.3 us
    all_to_all x1, local copies, waits for them, and re-layouts, body(): lax.all_to_all(train_inputs, 'dp', split_axis=0, concat_axis=1, tiled=True)  9.98 us
  transfers between devices with their start and end apart: 4, of which 3 were waited for; matrix products, arithmetic and copies ran while one was open for 7% of the time, Pallas kernels for 0%

commit v1 on v0

v1 whole, which is shorter than its diff:
```python
import functools

import jax
import jax.numpy as jnp
from jax import lax
from jax.experimental import pallas as pl
from jax.experimental.pallas import tpu as pltpu
from jax.sharding import PartitionSpec as P

SEQ = 128
CHUNK = 4
NT = (((1,), (1,)), ((), ()))
TN = (((0,), (0,)), ((), ()))
VMEM = pl.BlockSpec(memory_space=pltpu.VMEM)
HBM = pl.BlockSpec(memory_space=pl.ANY)
PARAMS = pltpu.CompilerParams(vmem_limit_bytes=32 * 2**20)


def axis_orders(n):
    bits = [1 << k for k in range(1, n.bit_length() - 1)]
    turn = len(bits) // 2
    return bits, bits[turn:] + bits[:turn]


def block_at(me, spot, keep, n):
    core = me % 2 if keep else 1 - me % 2
    even, odd = axis_orders(n)
    block = core
    for place, (bit_even, bit_odd) in enumerate(zip(even, odd, strict=True)):
        flip = 1 - (spot // (1 << (len(even) - 1 - place))) % 2
        for wanted, bit in ((0, bit_even), (1, bit_odd)):
            own = (me // bit) % 2
            value = own + flip - 2 * own * flip
            block = block + jnp.where(core == wanted, value * bit, 0)
    return block


def project_kernel(n, keep, ti, tg, qi, qg, wi, wo, out, ti_v, tg_v, qi_v, qg_v, wi_v, wo_v, sems, block_sems):
    me = lax.axis_index("dp")
    core = me % 2 if keep else 1 - me % 2
    rank = wi.shape[0]
    half = n // 2
    rows = ti.shape[0] // n
    qrows = qi.shape[0] // 2
    qspan = pl.ds(pl.multiple_of(core * qrows, qrows), qrows)
    copies = [
        pltpu.make_async_copy(wi, wi_v.at[pl.ds(rank, rank)], sems.at[0]),
        pltpu.make_async_copy(wo, wo_v.at[pl.ds(0, rank)], sems.at[1]),
        pltpu.make_async_copy(qi.at[qspan], qi_v, sems.at[2]),
        pltpu.make_async_copy(qg.at[qspan], qg_v, sems.at[3]),
    ]
    for copy in copies:
        copy.start()

    def block_copies(spot):
        block = block_at(me, spot, keep, n)
        source = pl.ds(pl.multiple_of(block * rows, rows), rows)
        target = pl.ds(pl.multiple_of(spot * rows, rows), rows)
        return (
            pltpu.make_async_copy(ti.at[source], ti_v.at[target], block_sems.at[0, spot]),
            pltpu.make_async_copy(tg.at[source], tg_v.at[target], block_sems.at[1, spot]),
        )

    def start(spot, carry):
        for copy in block_copies(spot):
            copy.start()
        return carry

    lax.fori_loop(0, half, start, 0, unroll=half <= 8)
    wi_v[pl.ds(0, rank), :] = jnp.zeros((rank, wi_v.shape[1]), wi_v.dtype)
    wo_v[pl.ds(rank, rank), :] = jnp.zeros((rank, wo_v.shape[1]), wo_v.dtype)
    for copy in copies:
        copy.wait()
    dot = lambda x, w: lax.dot_general(x, w[...], NT, preferred_element_type=jnp.float32)
    out[pl.ds(half * rows, qrows), :] = dot(qg_v[...], wo_v) + dot(qi_v[...], wi_v)

    def chunk(step, carry):
        for k in range(CHUNK):
            for copy in block_copies(step * CHUNK + k):
                copy.wait()
        span = pl.ds(pl.multiple_of(step * CHUNK * rows, CHUNK * rows), CHUNK * rows)
        out[span, :] = dot(tg_v[span, :], wo_v) + dot(ti_v[span, :], wi_v)
        return carry

    lax.fori_loop(0, half // CHUNK, chunk, 0, unroll=half <= 8)


def project(n, keep, ti, tg, qi, qg, wi, wo):
    rank, half = wi.shape[0], n // 2
    rows, qrows = ti.shape[0] // n, qi.shape[0] // 2
    bf = jnp.bfloat16
    scratch = [
        pltpu.VMEM((half * rows, ti.shape[1]), bf),
        pltpu.VMEM((half * rows, tg.shape[1]), bf),
        pltpu.VMEM((qrows, qi.shape[1]), bf),
        pltpu.VMEM((qrows, qg.shape[1]), bf),
        pltpu.VMEM((2 * rank, wi.shape[1]), bf),
        pltpu.VMEM((2 * rank, wo.shape[1]), bf),
        pltpu.SemaphoreType.DMA((4,)),
        pltpu.SemaphoreType.DMA((2, half)),
    ]
    total = half * rows + qrows
    flops = 2 * total * 2 * rank * (ti.shape[1] + tg.shape[1])
    return pl.pallas_call(
        functools.partial(project_kernel, n, keep),
        out_shape=jax.ShapeDtypeStruct((total, 2 * rank), jnp.float32),
        in_specs=[HBM] * 6,
        out_specs=VMEM,
        scratch_shapes=scratch,
        compiler_params=PARAMS,
        cost_estimate=pl.CostEstimate(flops=flops, bytes_accessed=total * 2 * (ti.shape[1] + tg.shape[1]), transcendentals=0),
        name="project_keep" if keep else "project_send",
    )(ti, tg, qi, qg, wi, wo)


def combine_kernel(held, query, got, send, keep):
    h = keep.shape[0]
    q = send.shape[0] - h
    send[pl.ds(0, h), :] = held[pl.ds(0, h), :] + got[pl.ds(0, h), :]
    keep[...] = held[pl.ds(h, h), :] + got[pl.ds(h, h), :]
    send[pl.ds(h, q), :] = query[pl.ds(query.shape[0] - q, q), :] + got[pl.ds(2 * h, q), :]


def combine(held, query, got, h, q):
    w = got.shape[1]
    return pl.pallas_call(
        combine_kernel,
        out_shape=(jax.ShapeDtypeStruct((h + q, w), jnp.float32), jax.ShapeDtypeStruct((h, w), jnp.float32)),
        in_specs=[VMEM] * 3,
        out_specs=(VMEM, VMEM),
        compiler_params=PARAMS,
        name="combine",
    )(held, query, got)


def finish_kernel(keep, query, got, own, own_query):
    h = keep.shape[0]
    q = own_query.shape[0]
    own[...] = (keep[...] + got[pl.ds(0, h), :]).astype(jnp.bfloat16)
    own_query[...] = (query[pl.ds(h, q), :] + got[pl.ds(h, q), :]).astype(jnp.bfloat16)


def finish(keep, query, got):
    h, w = keep.shape
    q = query.shape[0] - h
    return pl.pallas_call(
        finish_kernel,
        out_shape=(jax.ShapeDtypeStruct((h, w), jnp.bfloat16), jax.ShapeDtypeStruct((q, w), jnp.bfloat16)),
        in_specs=[VMEM] * 3,
        out_specs=(VMEM, VMEM),
        compiler_params=PARAMS,
        name="finish",
    )(keep, query, got)


def score_kernel(own, mine, other, scores):
    rank = own.shape[1] // 2
    scale = 1.0 / (SEQ * rank)
    core = lax.axis_index("dp") % 2

    def outer(ref, k):
        rows = ref[pl.ds(k * SEQ, SEQ), :]
        return lax.dot_general(rows[:, :rank], rows[:, rank:], TN, preferred_element_type=jnp.float32)

    count = mine.shape[0] // SEQ
    lane = lax.broadcasted_iota(jnp.int32, scores.shape, 1)
    row = lax.broadcasted_iota(jnp.int32, scores.shape, 0)
    result = jnp.zeros(scores.shape, jnp.float32)
    examples = [outer(own, e) for e in range(scores.shape[0])]
    for ref, side in ((mine, core), (other, 1 - core)):
        for k in range(count):
            grad = outer(ref, k)
            for e, example in enumerate(examples):
                value = jnp.sum(example * grad) * scale
                result = jnp.where((lane == side * count + k) & (row == e), value, result)
    scores[...] = result


def score(own, mine, other):
    shape = (own.shape[0] // SEQ, 2 * mine.shape[0] // SEQ)
    return pl.pallas_call(
        score_kernel,
        out_shape=jax.ShapeDtypeStruct(shape, jnp.float32),
        in_specs=[VMEM] * 3,
        out_specs=VMEM,
        compiler_params=PARAMS,
        name="score",
    )(own, mine, other)


def body(train_inputs, train_grads, query_inputs, query_grads, proj_in, proj_out):
    n = lax.axis_size("dp")
    args = (train_inputs, train_grads, query_inputs, query_grads, proj_in, proj_out)
    even, odd = axis_orders(n)
    swap = lambda x, be, bo: lax.ppermute(x, "dp", [(i, i ^ (bo if i % 2 else be)) for i in range(n)])
    send = project(n, False, *args)
    got = swap(send, 1, 1)
    held = project(n, True, *args)
    q = query_inputs.shape[0] // 2
    h = held.shape[0] - q
    query = held
    for be, bo in zip(even, odd, strict=True):
        h //= 2
        query, held = combine(held, query, got, h, q)
        got = swap(query, be, bo)
    own, mine = finish(held, query, got)
    other = swap(mine, 1, 1)
    return score(own, mine, other)


def solution(mesh):
    return jax.shard_map(
        body,
        mesh=mesh,
        in_specs=(
            P("groups", "dp"),
            P("groups", "dp"),
            P("groups", "dp"),
            P("groups", "dp"),
            P(None, "dp"),
            P(None, "dp"),
        ),
        out_specs=P(("groups", "dp"), None),
        check_vma=False,
    )
```

time: 314 us -> 53.4 us (0.17)
  waiting for transfers between devices: 183 us -> 19.9 us
  blocking collectives: 85.5 us -> 0 us
  Pallas kernels: 0 us -> 16.2 us
  between operations: 13.2 us -> 0.06 us
  matrix products: 10.4 us -> 0 us
  local copies, waits for them, and re-layouts: 15.6 us -> 8.99 us
    unnamed x4 -> x0, waiting for transfers between devices: 129 us -> none
    all_to_all x1 -> x0, blocking collectives: 54.9 us -> none  [body(): lax.all_to_all(train_grads, 'dp', split_axis=0, concat_axis=1, tiled=True)]
    all_gather x2 -> x0, waiting for transfers between devices: 54.6 us -> none  [the longest x1 32.3 us: body(): lax.all_gather(proj_out, 'dp', axis=1, tiled=True)]
    all_gather x1 -> x0, blocking collectives: 30.6 us -> none  [body(): pieces = lax.all_gather(piece, 'dp', axis=0, tiled=True)]
    ppermute x0 -> x5, waiting for transfers between devices: none -> 19.9 us  [body(): lax.ppermute(x, 'dp', [(i, i ^ (bo if i % 2 else be)) for i in range(n)])]
    pallas_call x0 -> x7, Pallas kernels: none -> 16.2 us  [the longest x2 15.1 us: project(): pl.pallas_call(functools.partial(project_kernel, n, keep), out_shape=jax....]
    all_to_all x2 -> x0, local copies, waits for them, and re-layouts: 13.9 us -> none  [the longest x1 9.98 us: body(): lax.all_to_all(train_inputs, 'dp', split_axis=0, concat_axis=1, tiled=True)]
    dot_general x6 -> x0, matrix products: 10.4 us -> none  [the longest x2 6.24 us: partial_proj(): lax.dot_general(inputs, proj_in, dims, preferred_element_type=jnp.float32)]
  transfers between devices with their start and end apart: 4 -> 5, of which waited for: 3 -> 4; matrix products, arithmetic and copies ran while one was open for 7% -> 0% of each run, Pallas kernels for 0% -> 14%
where the time goes in v1:
time: 53.4 us; the launch traced here: 53.1 us
  waiting for transfers between devices  19.9 us (37%)
  Pallas kernels  16.2 us (30%)
  local copies, waits for them, and re-layouts  8.99 us (17%)
  starting transfers between devices  7.93 us (15%)
    ppermute x5, waiting for transfers between devices, body(): lax.ppermute(x, 'dp', [(i, i ^ (bo if i % 2 else be)) for i in range(n)])  19.9 us
    pallas_call x2, Pallas kernels, project(): pl.pallas_call(functools.partial(project_kernel, n, keep), out_shape=jax....  15.1 us
    unnamed x12, local copies, waits for them, and re-layouts  8.99 us
    ppermute x5, starting transfers between devices, body(): lax.ppermute(x, 'dp', [(i, i ^ (bo if i % 2 else be)) for i in range(n)])  7.93 us
  transfers between devices with their start and end apart: 5, of which 4 were waited for; matrix products, arithmetic and copies ran while one was open for 0% of the time, Pallas kernels for 14%

profile of v1, /device:TPU:0, one launch (start us, length us, event | category | flops | bytes accessed | tf_op | source)
XLA Modules:
  0.0 53.1 jit_solution(9888662568818568897)
XLA Ops:
  0.0 0.0 copy-start
  0.0 3.1 %copy-done = bf16[2048,1792]{1,0:T(8,128)(2,1)S(1)} copy-done((bf16[2048,1792]{1,0:T(8,128)(2,1)S(1)}, bf16[2048,1792]{1,0:T(8,128)(2,1)}, u32[]{:S(2)}) %copy-start) | copy-done | bytes 7340056
  3.1 0.0 copy-start.1
  3.1 1.6 %copy-done.1 = bf16[2048,512]{1,0:T(8,128)(2,1)S(1)} copy-done((bf16[2048,512]{1,0:T(8,128)(2,1)S(1)}, bf16[2048,512]{1,0:T(8,128)(2,1)}, u32[]{:S(2)}) %copy-start.1) | copy-done | bytes 2097176
  4.7 0.0 copy-start.2
  4.7 1.5 %copy-done.2 = bf16[512,1792]{1,0:T(8,128)(2,1)S(1)} copy-done((bf16[512,1792]{1,0:T(8,128)(2,1)S(1)}, bf16[512,1792]{1,0:T(8,128)(2,1)}, u32[]{:S(2)}) %copy-start.2) | copy-done | bytes 1835032
  6.2 0.0 copy-start.3
  6.2 1.0 %copy-done.3 = bf16[512,512]{1,0:T(8,128)(2,1)S(1)} copy-done((bf16[512,512]{1,0:T(8,128)(2,1)S(1)}, bf16[512,512]{1,0:T(8,128)(2,1)}, u32[]{:S(2)}) %copy-start.3) | copy-done | bytes 524312
  7.2 0.0 copy-start.4
  7.2 0.9 %copy-done.4 = bf16[64,1792]{1,0:T(8,128)(2,1)S(1)} copy-done((bf16[64,1792]{1,0:T(8,128)(2,1)S(1)}, bf16[64,1792]{1,0:T(8,128)(2,1)}, u32[]{:S(2)}) %copy-start.4) | copy-done | bytes 229400
  8.2 0.0 copy-start.5
  8.2 0.8 %copy-done.5 = bf16[64,512]{1,0:T(8,128)(2,1)S(1)} copy-done((bf16[64,512]{1,0:T(8,128)(2,1)S(1)}, bf16[64,512]{1,0:T(8,128)(2,1)}, u32[]{:S(2)}) %copy-start.5) | copy-done | bytes 65560
  9.0 7.6 %project_send.1 = f32[1280,128]{1,0:T(8,128)S(1)} custom-call(bf16[2048,1792]{1,0:T(8,128)(2,1)S(1)} %copy-done, bf16[2048,512]{1,0:T(8,128)(2,1)S(1)} %copy-done.1, bf16[512,1792]{1,0:T(8,128)(2,1)S(1)} %copy-done.2, bf16[512,512]{1,0:T(8,128)(2,1)S(1)} %copy-done.3, bf16[64,1792]{1,0:T(8,128)(2,1)S(1)} %copy-done.4, bf16[64,512]{1,0:T(8,128)(2,1)S(1)} %copy-done.5), custom_call_target="tpu_custom_call" | custom-call | flops 754974720 | bytes 5898240 | tf_op jit(solution)/shard_map/project_send/pallas_call | solution.py:104
  16.6 0.5 collective-permute-start
  17.1 7.6 %project_keep.1.held.query = f32[1280,128]{1,0:T(8,128)S(1)} custom-call(bf16[2048,1792]{1,0:T(8,128)(2,1)S(1)} %copy-done, bf16[2048,512]{1,0:T(8,128)(2,1)S(1)} %copy-done.1, bf16[512,1792]{1,0:T(8,128)(2,1)S(1)} %copy-done.2, bf16[512,512]{1,0:T(8,128)(2,1)S(1)} %copy-done.3, bf16[64,1792]{1,0:T(8,128)(2,1)S(1)} %copy-done.4, bf16[64,512]{1,0:T(8,128)(2,1)S(1)} %copy-done.5), custom_call_target="tpu_custom_call" | custom-call | flops 754974720 | bytes 5898240 | tf_op jit(solution)/shard_map/project_keep/pallas_call | solution.py:104
  24.7 0.0 collective-permute-done.got
  24.7 0.1 combine.3
  24.8 2.6 %collective-permute-start.1 = (f32[768,128]{1,0:T(8,128)S(1)}, f32[768,128]{1,0:T(8,128)S(1)}, u32[]{:S(2)}, u32[]{:S(2)}) collective-permute-start(f32[768,128]{1,0:T(8,128)S(1)} %get-tuple-element.14.query), channel_id=1, source_target_pairs={{0,2},{1,5},{2,0},{3,7},{4,6},{5,1},{6,4},{7,3},{8,10},{9,13},{10,... | collective-permute-start | bytes 1179656 | tf_op jit(solution)/shard_map/ppermute | solution.py:195
  27.4 5.8 %collective-permute-done.1.got = f32[768,128]{1,0:T(8,128)S(1)} collective-permute-done((f32[768,128]{1,0:T(8,128)S(1)}, f32[768,128]{1,0:T(8,128)S(1)}, u32[]{:S(2)}, u32[]{:S(2)}) %collective-permute-start.1) | collective-permute-done | bytes 393248 | tf_op jit(solution)/shard_map/ppermute | solution.py:195
  33.2 2.1 %collective-permute-start.2 = (f32[512,128]{1,0:T(8,128)S(1)}, f32[512,128]{1,0:T(8,128)S(1)}, u32[]{:S(2)}, u32[]{:S(2)}) collective-permute-start(f32[512,128]{1,0:T(8,128)S(1)} %get-tuple-element.16.query), channel_id=1, source_target_pairs={{0,4},{1,9},{2,6},{3,11},{4,0},{5,13},{6,2},{7,15},{8,12},{9,1},{1... | collective-permute-start | bytes 786440 | tf_op jit(solution)/shard_map/ppermute | solution.py:195
  35.3 6.7 %collective-permute-done.2.got = f32[512,128]{1,0:T(8,128)S(1)} collective-permute-done((f32[512,128]{1,0:T(8,128)S(1)}, f32[512,128]{1,0:T(8,128)S(1)}, u32[]{:S(2)}, u32[]{:S(2)}) %collective-permute-start.2) | collective-permute-done | bytes 262176 | tf_op jit(solution)/shard_map/ppermute | solution.py:195
  42.1 2.6 %collective-permute-start.3 = (f32[384,128]{1,0:T(8,128)S(1)}, f32[384,128]{1,0:T(8,128)S(1)}, u32[]{:S(2)}, u32[]{:S(2)}) collective-permute-start(f32[384,128]{1,0:T(8,128)S(1)} %get-tuple-element.18.query), channel_id=1, source_target_pairs={{0,8},{1,3},{2,10},{3,1},{4,12},{5,7},{6,14},{7,5},{8,0},{9,11},{1... | collective-permute-start | bytes 589832 | tf_op jit(solution)/shard_map/ppermute | solution.py:195
  44.6 6.2 %collective-permute-done.3.got = f32[384,128]{1,0:T(8,128)S(1)} collective-permute-done((f32[384,128]{1,0:T(8,128)S(1)}, f32[384,128]{1,0:T(8,128)S(1)}, u32[]{:S(2)}, u32[]{:S(2)}) %collective-permute-start.3) | collective-permute-done | bytes 196640 | tf_op jit(solution)/shard_map/ppermute | solution.py:195
  50.8 0.1 collective-permute-start.4
  50.9 1.2 %collective-permute-done.4.other = bf16[256,128]{1,0:T(8,128)(2,1)S(1)} collective-permute-done((bf16[256,128]{1,0:T(8,128)(2,1)S(1)}, bf16[256,128]{1,0:T(8,128)(2,1)S(1)}, u32[]{:S(2)}, u32[]{:S(2)}) %collective-permute-start.4) | collective-permute-done | bytes 65568 | tf_op jit(solution)/shard_map/ppermute | solution.py:195
  52.1 0.9 %score.1 = f32[1,4]{1,0:T(1,128)} custom-call(bf16[128,128]{1,0:T(8,128)(2,1)S(1)} %get-tuple-element.19.own, bf16[256,128]{1,0:T(8,128)(2,1)S(1)} %get-tuple-element.20.mine, bf16[256,128]{1,0:T(8,128)(2,1)S(1)} %collective-permute-done.4.other), custom_call_target="tpu_custom_call" | custom-call | tf_op jit(solution)/shard_map/score/pallas_call | solution.py:181
  (3 shorter events, 0.1 us)
Async XLA Ops:
  0.0 3.1 %copy-start = (bf16[2048,1792]{1,0:T(8,128)(2,1)S(1)}, bf16[2048,1792]{1,0:T(8,128)(2,1)}, u32[]{:S(2)}) copy-start(bf16[2048,1792]{1,0:T(8,128)(2,1)} %ti.3) | copy-start | bytes 22020100
  3.1 1.6 %copy-start.1 = (bf16[2048,512]{1,0:T(8,128)(2,1)S(1)}, bf16[2048,512]{1,0:T(8,128)(2,1)}, u32[]{:S(2)}) copy-start(bf16[2048,512]{1,0:T(8,128)(2,1)} %tg.3) | copy-start | bytes 6291460
  4.7 1.5 %copy-start.2 = (bf16[512,1792]{1,0:T(8,128)(2,1)S(1)}, bf16[512,1792]{1,0:T(8,128)(2,1)}, u32[]{:S(2)}) copy-start(bf16[512,1792]{1,0:T(8,128)(2,1)} %qi.3) | copy-start | bytes 5505028
  6.2 1.0 %copy-start.3 = (bf16[512,512]{1,0:T(8,128)(2,1)S(1)}, bf16[512,512]{1,0:T(8,128)(2,1)}, u32[]{:S(2)}) copy-start(bf16[512,512]{1,0:T(8,128)(2,1)} %qg.3) | copy-start | bytes 1572868
  7.2 0.9 %copy-start.4 = (bf16[64,1792]{1,0:T(8,128)(2,1)S(1)}, bf16[64,1792]{1,0:T(8,128)(2,1)}, u32[]{:S(2)}) copy-start(bf16[64,1792]{1,0:T(8,128)(2,1)} %wi.3) | copy-start | bytes 688132
  8.2 0.8 %copy-start.5 = (bf16[64,512]{1,0:T(8,128)(2,1)S(1)}, bf16[64,512]{1,0:T(8,128)(2,1)}, u32[]{:S(2)}) copy-start(bf16[64,512]{1,0:T(8,128)(2,1)} %wo.3) | copy-start | bytes 196612
  16.6 8.1 %collective-permute-start = (f32[1280,128]{1,0:T(8,128)S(1)}, f32[1280,128]{1,0:T(8,128)S(1)}, u32[]{:S(2)}, u32[]{:S(2)}) collective-permute-start(f32[1280,128]{1,0:T(8,128)S(1)} %project_send.1), channel_id=1, source_target_pairs={{0,1},{1,0},{2,3},{3,2},{4,5},{5,4},{6,7},{7,6},{8,9},{9,8},{10,11... | collective-permute-start | bytes 1966088 | tf_op jit(solution)/shard_map/ppermute | solution.py:195
  24.8 8.4 %collective-permute-start.1 = (f32[768,128]{1,0:T(8,128)S(1)}, f32[768,128]{1,0:T(8,128)S(1)}, u32[]{:S(2)}, u32[]{:S(2)}) collective-permute-start(f32[768,128]{1,0:T(8,128)S(1)} %get-tuple-element.14.query), channel_id=1, source_target_pairs={{0,2},{1,5},{2,0},{3,7},{4,6},{5,1},{6,4},{7,3},{8,10},{9,13},{10,... | collective-permute-start | bytes 1179656 | tf_op jit(solution)/shard_map/ppermute | solution.py:195
  33.2 8.8 %collective-permute-start.2 = (f32[512,128]{1,0:T(8,128)S(1)}, f32[512,128]{1,0:T(8,128)S(1)}, u32[]{:S(2)}, u32[]{:S(2)}) collective-permute-start(f32[512,128]{1,0:T(8,128)S(1)} %get-tuple-element.16.query), channel_id=1, source_target_pairs={{0,4},{1,9},{2,6},{3,11},{4,0},{5,13},{6,2},{7,15},{8,12},{9,1},{1... | collective-permute-start | bytes 786440 | tf_op jit(solution)/shard_map/ppermute | solution.py:195
  42.1 8.7 %collective-permute-start.3 = (f32[384,128]{1,0:T(8,128)S(1)}, f32[384,128]{1,0:T(8,128)S(1)}, u32[]{:S(2)}, u32[]{:S(2)}) collective-permute-start(f32[384,128]{1,0:T(8,128)S(1)} %get-tuple-element.18.query), channel_id=1, source_target_pairs={{0,8},{1,3},{2,10},{3,1},{4,12},{5,7},{6,14},{7,5},{8,0},{9,11},{1... | collective-permute-start | bytes 589832 | tf_op jit(solution)/shard_map/ppermute | solution.py:195
  50.8 1.3 %collective-permute-start.4 = (bf16[256,128]{1,0:T(8,128)(2,1)S(1)}, bf16[256,128]{1,0:T(8,128)(2,1)S(1)}, u32[]{:S(2)}, u32[]{:S(2)}) collective-permute-start(bf16[256,128]{1,0:T(8,128)(2,1)S(1)} %get-tuple-element.20.mine), channel_id=1, source_target_pairs={{0,1},{1,0},{2,3},{3,2},{4,5},{5,4},{6,7},{7,6},{8,9},{9,8},{10,11... | collective-permute-start | bytes 196616 | tf_op jit(solution)/shard_map/ppermute | solution.py:195

commit v2 on v0

v2 whole, which is shorter than its diff:
```python
import functools

import jax
import jax.numpy as jnp
from jax import lax
from jax.experimental import pallas as pl
from jax.experimental.pallas import tpu as pltpu
from jax.sharding import PartitionSpec as P

SEQ = 128
NT = (((1,), (1,)), ((), ()))
VMEM = pl.BlockSpec(memory_space=pltpu.VMEM)
HBM = pl.BlockSpec(memory_space=pltpu.HBM)
PARAMS = pltpu.CompilerParams(vmem_limit_bytes=32 * 2**20)
LARGE = pltpu.CompilerParams(vmem_limit_bytes=60 * 2**20)


def axis_orders(n):
    bits = [1 << k for k in range(1, n.bit_length() - 1)]
    turn = len(bits) // 2
    return bits, bits[turn:] + bits[:turn]


def place_of(me, core, pair, n):
    even, odd = axis_orders(n)
    place = 0
    for bit_even, bit_odd in zip(even, odd, strict=True):
        differs = [(me // bit) % 2 != (pair // (bit // 2)) % 2 for bit in (bit_even, bit_odd)]
        stays = jnp.where(core == 0, jnp.where(differs[0], 0, 1), jnp.where(differs[1], 0, 1))
        place = 2 * place + stays
    return place


def pieces(width, step):
    step = step if width % step == 0 else width
    return [(at, step) for at in range(0, width, step)]


def project_kernel(n, keeps, step, train, query, proj, *refs):
    outs, (data, weights, sems, weight_sem) = refs[: len(keeps)], refs[len(keeps) :]
    me = lax.axis_index("dp")
    count, _, units = train.shape[:3]
    queries = query.shape[0] // 2
    rank, width = proj.shape
    spans = pieces(width, step)
    weight_copy = pltpu.make_async_copy(proj, weights, weight_sem)
    weight_copy.start()
    cores = [me % 2 if keep else 1 - me % 2 for keep in keeps]
    copies = []
    for i, core in enumerate(cores):
        for j, (at, size) in enumerate(spans):
            lanes = pl.ds(at, size)
            both = (
                pltpu.make_async_copy(
                    train.at[:, core, :, :, lanes], data.at[i, pl.ds(0, count), pl.ds(0, units), :, lanes], sems.at[0, i, j]
                ),
                pltpu.make_async_copy(
                    query.at[pl.ds(core * queries, queries), :, lanes],
                    data.at[i, pl.ds(count, queries), 0, :, lanes],
                    sems.at[1, i, j],
                ),
            )
            for copy in both:
                copy.start()
            copies.append((i, j, lanes, both))
    weight_copy.wait()
    total = (count + queries) * units * SEQ
    for i, j, lanes, both in copies:
        for copy in both:
            copy.wait()
        rows = data[i, :, :, :, lanes].reshape(total, lanes.size)
        term = lax.dot_general(weights[:, lanes], rows, NT, preferred_element_type=jnp.float32)
        partial = term if j == 0 else partial + term
        if j == len(spans) - 1:
            for unit in range(count * units):
                place = place_of(me, cores[i], unit // units, n) * units + unit % units
                outs[i][place] = partial[:, unit * SEQ : (unit + 1) * SEQ]
            for k in range(queries):
                unit = (count + k) * units
                outs[i][count * units + k] = partial[:, unit * SEQ : (unit + 1) * SEQ]


def project(n, keeps, step, train, query, proj):
    rank, width = proj.shape
    train = train.reshape(n // 2, 2, -1, SEQ, width)
    query = query.reshape(-1, SEQ, width)
    count, _, units = train.shape[:3]
    queries = query.shape[0] // 2
    number = len(keeps)
    spans = len(pieces(width, step))
    out = jax.ShapeDtypeStruct((count * units + queries, rank, SEQ), jnp.float32)
    rows = number * (count * units + queries) * SEQ
    return pl.pallas_call(
        functools.partial(project_kernel, n, keeps, step),
        out_shape=(out,) * number,
        in_specs=[HBM] * 3,
        out_specs=(VMEM,) * number,
        scratch_shapes=[
            pltpu.VMEM((number, count + queries, units, SEQ, width), jnp.bfloat16),
            pltpu.VMEM((rank, width), jnp.bfloat16),
            pltpu.SemaphoreType.DMA((2, number, spans)),
            pltpu.SemaphoreType.DMA,
        ],
        compiler_params=LARGE,
        cost_estimate=pl.CostEstimate(flops=2 * rows * rank * width, bytes_accessed=2 * rows * width, transcendentals=0),
        name="project",
    )(train, query, proj)


def combine_kernel(held, query, got, send, keep):
    h = keep.shape[0]
    q = send.shape[0] - h
    send[pl.ds(0, h)] = held[pl.ds(0, h)] + got[pl.ds(0, h)]
    keep[...] = held[pl.ds(h, h)] + got[pl.ds(h, h)]
    send[pl.ds(h, q)] = query[pl.ds(query.shape[0] - q, q)] + got[pl.ds(2 * h, q)]


def combine(held, query, got, h, q):
    tile = got.shape[1:]
    return pl.pallas_call(
        combine_kernel,
        out_shape=(jax.ShapeDtypeStruct((h + q,) + tile, jnp.float32), jax.ShapeDtypeStruct((h,) + tile, jnp.float32)),
        in_specs=[VMEM] * 3,
        out_specs=(VMEM, VMEM),
        compiler_params=PARAMS,
        name="combine",
    )(held, query, got)


def finish_kernel(keep, query, got, own, own_query):
    h = keep.shape[0]
    q = own_query.shape[0]
    own[...] = (keep[...] + got[pl.ds(0, h)]).astype(jnp.bfloat16)
    own_query[...] = (query[pl.ds(h, q)] + got[pl.ds(h, q)]).astype(jnp.bfloat16)


def finish(keep, query, got):
    tile = got.shape[1:]
    h = keep.shape[0]
    return pl.pallas_call(
        finish_kernel,
        out_shape=(
            jax.ShapeDtypeStruct((h,) + tile, jnp.bfloat16),
            jax.ShapeDtypeStruct((query.shape[0] - h,) + tile, jnp.bfloat16),
        ),
        in_specs=[VMEM] * 3,
        out_specs=(VMEM, VMEM),
        compiler_params=PARAMS,
        name="finish",
    )(keep, query, got)


def score_kernel(own_a, own_b, mine_a, mine_b, other_a, other_b, scores):
    core = lax.axis_index("dp") % 2
    count = mine_a.shape[0]
    scale = 1.0 / (SEQ * own_a.shape[1])

    def outer(a, b, k):
        return lax.dot_general(a[k], b[k], NT, preferred_element_type=jnp.float32)

    lane = lax.broadcasted_iota(jnp.int32, scores.shape, 1)
    row = lax.broadcasted_iota(jnp.int32, scores.shape, 0)
    result = jnp.zeros(scores.shape, jnp.float32)
    examples = [outer(own_a, own_b, e) for e in range(scores.shape[0])]
    for a, b, side in ((mine_a, mine_b, core), (other_a, other_b, 1 - core)):
        for k in range(count):
            grad = outer(a, b, k)
            for e, example in enumerate(examples):
                value = jnp.sum(example * grad) * scale
                result = jnp.where((lane == side * count + k) & (row == e), value, result)
    scores[...] = result


def score(*arrays):
    return pl.pallas_call(
        score_kernel,
        out_shape=jax.ShapeDtypeStruct((arrays[0].shape[0], 2 * arrays[2].shape[0]), jnp.float32),
        in_specs=[VMEM] * 6,
        out_specs=VMEM,
        compiler_params=PARAMS,
        name="score",
    )(*arrays)


def body(train_inputs, train_grads, query_inputs, query_grads, proj_in, proj_out):
    n = lax.axis_size("dp")
    even, odd = axis_orders(n)
    swap = lambda x, be, bo: lax.ppermute(x, "dp", [(i, i ^ (bo if i % 2 else be)) for i in range(n)])
    q = query_inputs.shape[0] // SEQ // 2

    def first(send, held):
        return swap(send, 1, 1), held, held

    send_a, held_a = project(n, (False, True), 256, train_grads, query_grads, proj_out)
    got_a = swap(send_a, 1, 1)
    (send_b,) = project(n, (False,), 256, train_inputs, query_inputs, proj_in)
    got_b = swap(send_b, 1, 1)
    (held_b,) = project(n, (True,), 256, train_inputs, query_inputs, proj_in)
    sides = [(held_a, held_a, got_a), (held_b, held_b, got_b)]
    h = held_a.shape[0] - q
    for be, bo in zip(even, odd, strict=True):
        h //= 2
        for s, (held, query, got) in enumerate(sides):
            query, held = combine(held, query, got, h, q)
            sides[s] = (held, query, swap(query, be, bo))
    (own_a, mine_a), (own_b, mine_b) = [finish(*side) for side in sides]
    other_a, other_b = swap(mine_a, 1, 1), swap(mine_b, 1, 1)
    return score(own_a, own_b, mine_a, mine_b, other_a, other_b)


def solution(mesh):
    return jax.shard_map(
        body,
        mesh=mesh,
        in_specs=(
            P("groups", "dp"),
            P("groups", "dp"),
            P("groups", "dp"),
            P("groups", "dp"),
            P(None, "dp"),
            P(None, "dp"),
        ),
        out_specs=P(("groups", "dp"), None),
        check_vma=False,
    )
```

time: 314 us -> 35.5 us (0.11)
  waiting for transfers between devices: 183 us -> 7.34 us
  blocking collectives: 85.5 us -> 0 us
  local copies, waits for them, and re-layouts: 15.6 us -> 0.97 us
  between operations: 13.2 us -> 0.08 us
  Pallas kernels: 0 us -> 12.7 us
  matrix products: 10.4 us -> 0 us
  starting transfers between devices: 5.4 us -> 14.2 us
    unnamed x4 -> x0, waiting for transfers between devices: 129 us -> none
    all_to_all x1 -> x0, blocking collectives: 54.9 us -> none  [body(): lax.all_to_all(train_grads, 'dp', split_axis=0, concat_axis=1, tiled=True)]
    all_gather x2 -> x0, waiting for transfers between devices: 54.6 us -> none  [the longest x1 32.3 us: body(): lax.all_gather(proj_out, 'dp', axis=1, tiled=True)]
    all_gather x1 -> x0, blocking collectives: 30.6 us -> none  [body(): pieces = lax.all_gather(piece, 'dp', axis=0, tiled=True)]
    ppermute x0 -> x10, starting transfers between devices: none -> 14.2 us  [body(): lax.ppermute(x, 'dp', [(i, i ^ (bo if i % 2 else be)) for i in range(n)])]
    all_to_all x2 -> x0, local copies, waits for them, and re-layouts: 13.9 us -> none  [the longest x1 9.98 us: body(): lax.all_to_all(train_inputs, 'dp', split_axis=0, concat_axis=1, tiled=True)]
    pallas_call x0 -> x12, Pallas kernels: none -> 12.7 us  [the longest x3 11.7 us: project(): pl.pallas_call(functools.partial(project_kernel, n, keeps, step), out_sha...]
    dot_general x6 -> x0, matrix products: 10.4 us -> none  [the longest x2 6.24 us: partial_proj(): lax.dot_general(inputs, proj_in, dims, preferred_element_type=jnp.float32)]
  transfers between devices with their start and end apart: 4 -> 10, of which waited for: 3 -> 5; matrix products, arithmetic and copies ran while one was open for 7% -> 0% of each run, Pallas kernels for 0% -> 24%
where the time goes in v2:
time: 35.5 us; the launch traced here: 35.3 us
  starting transfers between devices  14.2 us (40%)
  Pallas kernels  12.7 us (36%)
  waiting for transfers between devices  7.34 us (21%)
  local copies, waits for them, and re-layouts  0.97 us (3%)
    ppermute x10, starting transfers between devices, body(): lax.ppermute(x, 'dp', [(i, i ^ (bo if i % 2 else be)) for i in range(n)])  14.2 us
    pallas_call x3, Pallas kernels, project(): pl.pallas_call(functools.partial(project_kernel, n, keeps, step), out_sha...  11.7 us
    ppermute x10, waiting for transfers between devices, body(): lax.ppermute(x, 'dp', [(i, i ^ (bo if i % 2 else be)) for i in range(n)])  7.34 us
    unnamed x4, local copies, waits for them, and re-layouts  0.97 us
    pallas_call x1, Pallas kernels, score(): pl.pallas_call(score_kernel, out_shape=jax.ShapeDtypeStruct((arrays[0].sh...  0.81 us
  transfers between devices with their start and end apart: 10, of which 5 were waited for; matrix products, arithmetic and copies ran while one was open for 0% of the time, Pallas kernels for 24%

profile of v2, /device:TPU:0, one launch (start us, length us, event | category | flops | bytes accessed | tf_op | source)
XLA Modules:
  0.0 35.3 jit_solution(9626673867220813089)
XLA Ops:
  0.0 3.3 %project.3 = (f32[10,64,128]{2,1,0:T(8,128)}, f32[10,64,128]{2,1,0:T(8,128)}) custom-call(bf16[8,2,1,128,512]{4,3,2,1,0:T(8,128)(2,1)} %bitcast.8, bf16[4,128,512]{2,1,0:T(8,128)(2,1)} %bitcast.9, bf16[64,512]{1,0:T(8,128)(2,1)} %proj.3), custom_call_target="tpu_custom_call" | custom-call | flops 167772160 | bytes 2621440 | tf_op jit(solution)/shard_map/project/pallas_call | solution.py:93
  3.3 0.5 %collective-permute-start = (f32[10,64,128]{2,1,0:T(8,128)}, f32[10,64,128]{2,1,0:T(8,128)S(1)}, u32[]{:S(2)}, u32[]{:S(2)}) collective-permute-start(f32[10,64,128]{2,1,0:T(8,128)} %get-tuple-element.24), channel_id=1, source_target_pairs={{0,1},{1,0},{2,3},{3,2},{4,5},{5,4},{6,7},{7,6},{8,9},{9,8},{10,11... | collective-permute-start | bytes 983048 | tf_op jit(solution)/shard_map/ppermute | solution.py:188
  3.8 0.0 copy-start.1
  3.9 4.2 %project.5 = f32[10,64,128]{2,1,0:T(8,128)} custom-call(bf16[8,2,1,128,1792]{4,3,2,1,0:T(8,128)(2,1)} %bitcast.4, bf16[4,128,1792]{2,1,0:T(8,128)(2,1)} %bitcast.6, bf16[64,1792]{1,0:T(8,128)(2,1)} %proj.5), custom_call_target="tpu_custom_call" | custom-call | flops 293601280 | bytes 4587520 | tf_op jit(solution)/shard_map/project/pallas_call | solution.py:93
  8.1 0.1 collective-permute-start.4
  8.2 0.0 collective-permute-done.got
  8.2 0.0 copy-done.1
  8.3 3.0 %collective-permute-start.1 = (f32[6,64,128]{2,1,0:T(8,128)S(1)}, f32[6,64,128]{2,1,0:T(8,128)S(1)}, u32[]{:S(2)}, u32[]{:S(2)}) collective-permute-start(f32[6,64,128]{2,1,0:T(8,128)S(1)} %get-tuple-element.26.query), channel_id=1, source_target_pairs={{0,2},{1,5},{2,0},{3,7},{4,6},{5,1},{6,4},{7,3},{8,10},{9,13},{10,... | collective-permute-start | bytes 589832 | tf_op jit(solution)/shard_map/ppermute | solution.py:188
  11.3 4.2 %project.4.held.query = f32[10,64,128]{2,1,0:T(8,128)} custom-call(bf16[8,2,1,128,1792]{4,3,2,1,0:T(8,128)(2,1)} %bitcast.5, bf16[4,128,1792]{2,1,0:T(8,128)(2,1)} %bitcast.7, bf16[64,1792]{1,0:T(8,128)(2,1)} %proj.5), custom_call_target="tpu_custom_call" | custom-call | flops 293601280 | bytes 4587520 | tf_op jit(solution)/shard_map/project/pallas_call | solution.py:93
  15.5 0.0 collective-permute-done.4.got
  15.5 0.0 copy-start
  15.5 1.0 %copy-done = f32[10,64,128]{2,1,0:T(8,128)S(1)} copy-done((f32[10,64,128]{2,1,0:T(8,128)S(1)}, f32[10,64,128]{2,1,0:T(8,128)}, u32[]{:S(2)}) %copy-start) | copy-done | bytes 327704
  16.5 0.1 collective-permute-start.5
  16.6 0.0 collective-permute-done.1.got
  16.6 2.1 %collective-permute-start.2 = (f32[4,64,128]{2,1,0:T(8,128)S(1)}, f32[4,64,128]{2,1,0:T(8,128)S(1)}, u32[]{:S(2)}, u32[]{:S(2)}) collective-permute-start(f32[4,64,128]{2,1,0:T(8,128)S(1)} %get-tuple-element.28.query), channel_id=1, source_target_pairs={{0,4},{1,9},{2,6},{3,11},{4,0},{5,13},{6,2},{7,15},{8,12},{9,1},{1... | collective-permute-start | bytes 393224 | tf_op jit(solution)/shard_map/ppermute | solution.py:188
  18.7 3.5 %collective-permute-done.5.got = f32[6,64,128]{2,1,0:T(8,128)S(1)} collective-permute-done((f32[6,64,128]{2,1,0:T(8,128)S(1)}, f32[6,64,128]{2,1,0:T(8,128)S(1)}, u32[]{:S(2)}, u32[]{:S(2)}) %collective-permute-start.5) | collective-permute-done | bytes 196640 | tf_op jit(solution)/shard_map/ppermute | solution.py:188
  22.3 1.6 %collective-permute-start.6 = (f32[4,64,128]{2,1,0:T(8,128)S(1)}, f32[4,64,128]{2,1,0:T(8,128)S(1)}, u32[]{:S(2)}, u32[]{:S(2)}) collective-permute-start(f32[4,64,128]{2,1,0:T(8,128)S(1)} %get-tuple-element.35.query), channel_id=1, source_target_pairs={{0,4},{1,9},{2,6},{3,11},{4,0},{5,13},{6,2},{7,15},{8,12},{9,1},{1... | collective-permute-start | bytes 393224 | tf_op jit(solution)/shard_map/ppermute | solution.py:188
  23.9 0.0 collective-permute-done.2.got
  23.9 2.7 %collective-permute-start.3 = (f32[3,64,128]{2,1,0:T(8,128)S(1)}, f32[3,64,128]{2,1,0:T(8,128)S(1)}, u32[]{:S(2)}, u32[]{:S(2)}) collective-permute-start(f32[3,64,128]{2,1,0:T(8,128)S(1)} %get-tuple-element.30.query), channel_id=1, source_target_pairs={{0,8},{1,3},{2,10},{3,1},{4,12},{5,7},{6,14},{7,5},{8,0},{9,11},{1... | collective-permute-start | bytes 294920 | tf_op jit(solution)/shard_map/ppermute | solution.py:188
  26.6 0.7 %collective-permute-done.6.got = f32[4,64,128]{2,1,0:T(8,128)S(1)} collective-permute-done((f32[4,64,128]{2,1,0:T(8,128)S(1)}, f32[4,64,128]{2,1,0:T(8,128)S(1)}, u32[]{:S(2)}, u32[]{:S(2)}) %collective-permute-start.6) | collective-permute-done | bytes 131104 | tf_op jit(solution)/shard_map/ppermute | solution.py:188
  27.3 2.6 %collective-permute-start.7 = (f32[3,64,128]{2,1,0:T(8,128)S(1)}, f32[3,64,128]{2,1,0:T(8,128)S(1)}, u32[]{:S(2)}, u32[]{:S(2)}) collective-permute-start(f32[3,64,128]{2,1,0:T(8,128)S(1)} %get-tuple-element.37.query), channel_id=1, source_target_pairs={{0,8},{1,3},{2,10},{3,1},{4,12},{5,7},{6,14},{7,5},{8,0},{9,11},{1... | collective-permute-start | bytes 294920 | tf_op jit(solution)/shard_map/ppermute | solution.py:188
  30.0 1.0 %collective-permute-done.3.got = f32[3,64,128]{2,1,0:T(8,128)S(1)} collective-permute-done((f32[3,64,128]{2,1,0:T(8,128)S(1)}, f32[3,64,128]{2,1,0:T(8,128)S(1)}, u32[]{:S(2)}, u32[]{:S(2)}) %collective-permute-start.3) | collective-permute-done | bytes 98336 | tf_op jit(solution)/shard_map/ppermute | solution.py:188
  30.9 0.7 %collective-permute-start.8 = (bf16[2,64,128]{2,1,0:T(8,128)(2,1)S(1)}, bf16[2,64,128]{2,1,0:T(8,128)(2,1)S(1)}, u32[]{:S(2)}, u32[]{:S(2)}) collective-permute-start(bf16[2,64,128]{2,1,0:T(8,128)(2,1)S(1)} %get-tuple-element.39.mine_a), channel_id=1, source_target_pairs={{0,1},{1,0},{2,3},{3,2},{4,5},{5,4},{6,7},{7,6},{8,9},{9,8},{10,11... | collective-permute-start | bytes 98312 | tf_op jit(solution)/shard_map/ppermute | solution.py:188
  31.6 1.3 %collective-permute-done.7.got = f32[3,64,128]{2,1,0:T(8,128)S(1)} collective-permute-done((f32[3,64,128]{2,1,0:T(8,128)S(1)}, f32[3,64,128]{2,1,0:T(8,128)S(1)}, u32[]{:S(2)}, u32[]{:S(2)}) %collective-permute-start.7) | collective-permute-done | bytes 98336 | tf_op jit(solution)/shard_map/ppermute | solution.py:188
  32.9 0.7 %collective-permute-start.9 = (bf16[2,64,128]{2,1,0:T(8,128)(2,1)S(1)}, bf16[2,64,128]{2,1,0:T(8,128)(2,1)S(1)}, u32[]{:S(2)}, u32[]{:S(2)}) collective-permute-start(bf16[2,64,128]{2,1,0:T(8,128)(2,1)S(1)} %get-tuple-element.40.mine_b), channel_id=1, source_target_pairs={{0,1},{1,0},{2,3},{3,2},{4,5},{5,4},{6,7},{7,6},{8,9},{9,8},{10,11... | collective-permute-start | bytes 98312 | tf_op jit(solution)/shard_map/ppermute | solution.py:188
  33.6 0.0 collective-permute-done.8.other_a
  33.6 0.9 %collective-permute-done.9.other_b = bf16[2,64,128]{2,1,0:T(8,128)(2,1)S(1)} collective-permute-done((bf16[2,64,128]{2,1,0:T(8,128)(2,1)S(1)}, bf16[2,64,128]{2,1,0:T(8,128)(2,1)S(1)}, u32[]{:S(2)}, u32[]{:S(2)}) %collective-permute-start.9) | collective-permute-done | bytes 32800 | tf_op jit(solution)/shard_map/ppermute | solution.py:188
  34.5 0.8 %score.1 = f32[1,4]{1,0:T(1,128)} custom-call(bf16[1,64,128]{2,1,0:T(8,128)(2,1)S(1)} %get-tuple-element.31.own_a, bf16[1,64,128]{2,1,0:T(8,128)(2,1)S(1)} %get-tuple-element.38.own_b, bf16[2,64,128]{2,1,0:T(8,128)(2,1)S(1)} %get-tuple-element.39.mine_a, bf16[2,64,128]{2,1,0:T(8,128)(2,1)S(1)} %get-tuple-element.40.mine_b, ...), custom_call_target="tpu_custom_call" | custom-call | tf_op jit(solution)/shard_map/score/pallas_call | solution.py:175
  (8 shorter events, 0.2 us)
Async XLA Ops:
  3.3 4.9 %collective-permute-start = (f32[10,64,128]{2,1,0:T(8,128)}, f32[10,64,128]{2,1,0:T(8,128)S(1)}, u32[]{:S(2)}, u32[]{:S(2)}) collective-permute-start(f32[10,64,128]{2,1,0:T(8,128)} %get-tuple-element.24), channel_id=1, source_target_pairs={{0,1},{1,0},{2,3},{3,2},{4,5},{5,4},{6,7},{7,6},{8,9},{9,8},{10,11... | collective-permute-start | bytes 983048 | tf_op jit(solution)/shard_map/ppermute | solution.py:188
  3.8 4.4 %copy-start.1 = (f32[10,64,128]{2,1,0:T(8,128)S(1)}, f32[10,64,128]{2,1,0:T(8,128)}, u32[]{:S(2)}) copy-start(f32[10,64,128]{2,1,0:T(8,128)} %get-tuple-element.23.held.query) | copy-start | bytes 983044
  8.1 7.4 %collective-permute-start.4 = (f32[10,64,128]{2,1,0:T(8,128)}, f32[10,64,128]{2,1,0:T(8,128)S(1)}, u32[]{:S(2)}, u32[]{:S(2)}) collective-permute-start(f32[10,64,128]{2,1,0:T(8,128)} %project.5), channel_id=1, source_target_pairs={{0,1},{1,0},{2,3},{3,2},{4,5},{5,4},{6,7},{7,6},{8,9},{9,8},{10,11... | collective-permute-start | bytes 983048 | tf_op jit(solution)/shard_map/ppermute | solution.py:188
  8.3 8.3 %collective-permute-start.1 = (f32[6,64,128]{2,1,0:T(8,128)S(1)}, f32[6,64,128]{2,1,0:T(8,128)S(1)}, u32[]{:S(2)}, u32[]{:S(2)}) collective-permute-start(f32[6,64,128]{2,1,0:T(8,128)S(1)} %get-tuple-element.26.query), channel_id=1, source_target_pairs={{0,2},{1,5},{2,0},{3,7},{4,6},{5,1},{6,4},{7,3},{8,10},{9,13},{10,... | collective-permute-start | bytes 589832 | tf_op jit(solution)/shard_map/ppermute | solution.py:188
  15.5 1.0 %copy-start = (f32[10,64,128]{2,1,0:T(8,128)S(1)}, f32[10,64,128]{2,1,0:T(8,128)}, u32[]{:S(2)}) copy-start(f32[10,64,128]{2,1,0:T(8,128)} %project.4.held.query) | copy-start | bytes 983044
  16.5 5.7 %collective-permute-start.5 = (f32[6,64,128]{2,1,0:T(8,128)S(1)}, f32[6,64,128]{2,1,0:T(8,128)S(1)}, u32[]{:S(2)}, u32[]{:S(2)}) collective-permute-start(f32[6,64,128]{2,1,0:T(8,128)S(1)} %get-tuple-element.33.query), channel_id=1, source_target_pairs={{0,2},{1,5},{2,0},{3,7},{4,6},{5,1},{6,4},{7,3},{8,10},{9,13},{10,... | collective-permute-start | bytes 589832 | tf_op jit(solution)/shard_map/ppermute | solution.py:188
  16.6 7.3 %collective-permute-start.2 = (f32[4,64,128]{2,1,0:T(8,128)S(1)}, f32[4,64,128]{2,1,0:T(8,128)S(1)}, u32[]{:S(2)}, u32[]{:S(2)}) collective-permute-start(f32[4,64,128]{2,1,0:T(8,128)S(1)} %get-tuple-element.28.query), channel_id=1, source_target_pairs={{0,4},{1,9},{2,6},{3,11},{4,0},{5,13},{6,2},{7,15},{8,12},{9,1},{1... | collective-permute-start | bytes 393224 | tf_op jit(solution)/shard_map/ppermute | solution.py:188
  22.3 5.1 %collective-permute-start.6 = (f32[4,64,128]{2,1,0:T(8,128)S(1)}, f32[4,64,128]{2,1,0:T(8,128)S(1)}, u32[]{:S(2)}, u32[]{:S(2)}) collective-permute-start(f32[4,64,128]{2,1,0:T(8,128)S(1)} %get-tuple-element.35.query), channel_id=1, source_target_pairs={{0,4},{1,9},{2,6},{3,11},{4,0},{5,13},{6,2},{7,15},{8,12},{9,1},{1... | collective-permute-start | bytes 393224 | tf_op jit(solution)/shard_map/ppermute | solution.py:188
  23.9 7.0 %collective-permute-start.3 = (f32[3,64,128]{2,1,0:T(8,128)S(1)}, f32[3,64,128]{2,1,0:T(8,128)S(1)}, u32[]{:S(2)}, u32[]{:S(2)}) collective-permute-start(f32[3,64,128]{2,1,0:T(8,128)S(1)} %get-tuple-element.30.query), channel_id=1, source_target_pairs={{0,8},{1,3},{2,10},{3,1},{4,12},{5,7},{6,14},{7,5},{8,0},{9,11},{1... | collective-permute-start | bytes 294920 | tf_op jit(solution)/shard_map/ppermute | solution.py:188
  27.3 5.6 %collective-permute-start.7 = (f32[3,64,128]{2,1,0:T(8,128)S(1)}, f32[3,64,128]{2,1,0:T(8,128)S(1)}, u32[]{:S(2)}, u32[]{:S(2)}) collective-permute-start(f32[3,64,128]{2,1,0:T(8,128)S(1)} %get-tuple-element.37.query), channel_id=1, source_target_pairs={{0,8},{1,3},{2,10},{3,1},{4,12},{5,7},{6,14},{7,5},{8,0},{9,11},{1... | collective-permute-start | bytes 294920 | tf_op jit(solution)/shard_map/ppermute | solution.py:188
  30.9 2.7 %collective-permute-start.8 = (bf16[2,64,128]{2,1,0:T(8,128)(2,1)S(1)}, bf16[2,64,128]{2,1,0:T(8,128)(2,1)S(1)}, u32[]{:S(2)}, u32[]{:S(2)}) collective-permute-start(bf16[2,64,128]{2,1,0:T(8,128)(2,1)S(1)} %get-tuple-element.39.mine_a), channel_id=1, source_target_pairs={{0,1},{1,0},{2,3},{3,2},{4,5},{5,4},{6,7},{7,6},{8,9},{9,8},{10,11... | collective-permute-start | bytes 98312 | tf_op jit(solution)/shard_map/ppermute | solution.py:188
  32.9 1.6 %collective-permute-start.9 = (bf16[2,64,128]{2,1,0:T(8,128)(2,1)S(1)}, bf16[2,64,128]{2,1,0:T(8,128)(2,1)S(1)}, u32[]{:S(2)}, u32[]{:S(2)}) collective-permute-start(bf16[2,64,128]{2,1,0:T(8,128)(2,1)S(1)} %get-tuple-element.40.mine_b), channel_id=1, source_target_pairs={{0,1},{1,0},{2,3},{3,2},{4,5},{5,4},{6,7},{7,6},{8,9},{9,8},{10,11... | collective-permute-start | bytes 98312 | tf_op jit(solution)/shard_map/ppermute | solution.py:188

commit v3 on v2

--- a/solution.py
+++ b/solution.py
@@ -12,7 +12,7 @@
 VMEM = pl.BlockSpec(memory_space=pltpu.VMEM)
 HBM = pl.BlockSpec(memory_space=pltpu.HBM)
 PARAMS = pltpu.CompilerParams(vmem_limit_bytes=32 * 2**20)
-LARGE = pltpu.CompilerParams(vmem_limit_bytes=60 * 2**20)
+LARGE = pltpu.CompilerParams(vmem_limit_bytes=48 * 2**20)
 
 
 def axis_orders(n):
@@ -31,80 +31,79 @@
     return place
 
 
-def pieces(width, step):
-    step = step if width % step == 0 else width
-    return [(at, step) for at in range(0, width, step)]
-
-
-def project_kernel(n, keeps, step, train, query, proj, *refs):
-    outs, (data, weights, sems, weight_sem) = refs[: len(keeps)], refs[len(keeps) :]
+def groups(count, size):
+    return [(at, min(size, count - at)) for at in range(0, count, size)]
+
+
+def project_kernel(n, sizes, *refs):
+    sides = [refs[3 * i : 3 * i + 3] for i in range(2)]
+    outs = [refs[6 + 2 * i : 8 + 2 * i] for i in range(2)]
+    buffers = [refs[10 + 3 * i : 13 + 3 * i] for i in range(2)]
+    sems = refs[16]
     me = lax.axis_index("dp")
-    count, _, units = train.shape[:3]
-    queries = query.shape[0] // 2
-    rank, width = proj.shape
-    spans = pieces(width, step)
-    weight_copy = pltpu.make_async_copy(proj, weights, weight_sem)
-    weight_copy.start()
-    cores = [me % 2 if keep else 1 - me % 2 for keep in keeps]
-    copies = []
-    for i, core in enumerate(cores):
-        for j, (at, size) in enumerate(spans):
-            lanes = pl.ds(at, size)
-            both = (
-                pltpu.make_async_copy(
-                    train.at[:, core, :, :, lanes], data.at[i, pl.ds(0, count), pl.ds(0, units), :, lanes], sems.at[0, i, j]
-                ),
-                pltpu.make_async_copy(
-                    query.at[pl.ds(core * queries, queries), :, lanes],
-                    data.at[i, pl.ds(count, queries), 0, :, lanes],
-                    sems.at[1, i, j],
-                ),
-            )
-            for copy in both:
-                copy.start()
-            copies.append((i, j, lanes, both))
-    weight_copy.wait()
-    total = (count + queries) * units * SEQ
-    for i, j, lanes, both in copies:
-        for copy in both:
+    mine = me % 2
+    pending = []
+    for side, (whole, held) in enumerate(zip(sides, buffers, strict=True)):
+        count = whole[0].shape[0]
+        copies = [
+            pltpu.make_async_copy(whole[2], held[2], sems.at[side, 0]),
+            pltpu.make_async_copy(whole[1], held[1], sems.at[side, 1]),
+        ]
+        spans = groups(count, sizes[side])
+        for j, (at, k) in enumerate(spans):
+            copies.append(pltpu.make_async_copy(whole[0].at[pl.ds(at, k)], held[0].at[pl.ds(at, k)], sems.at[side, 2 + j]))
+        for copy in copies:
+            copy.start()
+        pending.append((copies, spans))
+    places = {}
+    for (copies, spans), (train, query, proj), out in zip(pending, buffers, outs, strict=True):
+        count, _, units = train.shape[:3]
+        queries = query.shape[0] // 2
+        copies[0].wait()
+        copies[1].wait()
+
+        def dot(rows):
+            rows = rows.reshape(-1, rows.shape[-1])
+            return lax.dot_general(proj[...], rows, NT, preferred_element_type=jnp.float32)
+
+        for half, core in enumerate((1 - mine, mine)):
+            part = dot(query[pl.ds(core * queries, queries)])
+            for k in range(queries):
+                out[half][count * units + k] = part[:, k * SEQ : (k + 1) * SEQ]
+        for copy, (at, k) in zip(copies[2:], spans, strict=True):
             copy.wait()
-        rows = data[i, :, :, :, lanes].reshape(total, lanes.size)
-        term = lax.dot_general(weights[:, lanes], rows, NT, preferred_element_type=jnp.float32)
-        partial = term if j == 0 else partial + term
-        if j == len(spans) - 1:
-            for unit in range(count * units):
-                place = place_of(me, cores[i], unit // units, n) * units + unit % units
-                outs[i][place] = partial[:, unit * SEQ : (unit + 1) * SEQ]
-            for k in range(queries):
-                unit = (count + k) * units
-                outs[i][count * units + k] = partial[:, unit * SEQ : (unit + 1) * SEQ]
-
-
-def project(n, keeps, step, train, query, proj):
-    rank, width = proj.shape
-    train = train.reshape(n // 2, 2, -1, SEQ, width)
-    query = query.reshape(-1, SEQ, width)
-    count, _, units = train.shape[:3]
-    queries = query.shape[0] // 2
-    number = len(keeps)
-    spans = len(pieces(width, step))
-    out = jax.ShapeDtypeStruct((count * units + queries, rank, SEQ), jnp.float32)
-    rows = number * (count * units + queries) * SEQ
-    return pl.pallas_call(
-        functools.partial(project_kernel, n, keeps, step),
-        out_shape=(out,) * number,
-        in_specs=[HBM] * 3,
-        out_specs=(VMEM,) * number,
-        scratch_shapes=[
-            pltpu.VMEM((number, count + queries, units, SEQ, width), jnp.bfloat16),
-            pltpu.VMEM((rank, width), jnp.bfloat16),
-            pltpu.SemaphoreType.DMA((2, number, spans)),
-            pltpu.SemaphoreType.DMA,
-        ],
+            for half, core in enumerate((1 - mine, mine)):
+                part = dot(train[pl.ds(at, k), core])
+                for i in range(k):
+                    if (half, at + i) not in places:
+                        places[half, at + i] = place_of(me, core, at + i, n) * units
+                    for u in range(units):
+                        unit = i * units + u
+                        out[half][places[half, at + i] + u] = part[:, unit * SEQ : (unit + 1) * SEQ]
+
+
+def project(n, sizes, *sides):
+    views, outs, scratch, flops, moved = [], [], [], 0, 0
+    for train, query, proj in sides:
+        rank, width = proj.shape
+        views += [pltpu.with_memory_space_constraint(v, pltpu.HBM) for v in (train.reshape(n // 2, 2, -1, SEQ, width), query.reshape(-1, SEQ, width), proj)]
+        units, queries = views[-3].shape[2], views[-2].shape[0] // 2
+        outs += [jax.ShapeDtypeStruct((n // 2 * units + queries, rank, SEQ), jnp.float32)] * 2
+        scratch += [pltpu.VMEM(view.shape, view.dtype) for view in views[-3:]]
+        rows = train.shape[0] + query.shape[0]
+        flops += 2 * rows * rank * width
+        moved += 2 * rows * width
+    scratch.append(pltpu.SemaphoreType.DMA((2, 2 + max(len(groups(n // 2, size)) for size in sizes))))
+    return pl.pallas_call(
+        functools.partial(project_kernel, n, sizes),
+        out_shape=tuple(outs),
+        in_specs=[HBM] * 6,
+        out_specs=(VMEM,) * 4,
+        scratch_shapes=scratch,
         compiler_params=LARGE,
-        cost_estimate=pl.CostEstimate(flops=2 * rows * rank * width, bytes_accessed=2 * rows * width, transcendentals=0),
+        cost_estimate=pl.CostEstimate(flops=flops, bytes_accessed=moved, transcendentals=0),
         name="project",
-    )(train, query, proj)
+    )(*views)
 
 
 def combine_kernel(held, query, got, send, keep):
@@ -187,16 +186,9 @@
     even, odd = axis_orders(n)
     swap = lambda x, be, bo: lax.ppermute(x, "dp", [(i, i ^ (bo if i % 2 else be)) for i in range(n)])
     q = query_inputs.shape[0] // SEQ // 2
-
-    def first(send, held):
-        return swap(send, 1, 1), held, held
-
-    send_a, held_a = project(n, (False, True), 256, train_grads, query_grads, proj_out)
-    got_a = swap(send_a, 1, 1)
-    (send_b,) = project(n, (False,), 256, train_inputs, query_inputs, proj_in)
-    got_b = swap(send_b, 1, 1)
-    (held_b,) = project(n, (True,), 256, train_inputs, query_inputs, proj_in)
-    sides = [(held_a, held_a, got_a), (held_b, held_b, got_b)]
+    sides = ((train_grads, query_grads, proj_out), (train_inputs, query_inputs, proj_in))
+    send_a, held_a, send_b, held_b = project(n, (4, 2), *sides)
+    sides = [(held_a, held_a, swap(send_a, 1, 1)), (held_b, held_b, swap(send_b, 1, 1))]
     h = held_a.shape[0] - q
     for be, bo in zip(even, odd, strict=True):
         h //= 2

time: 35.5 us -> 31.2 us (0.88)
  Pallas kernels: 12.7 us -> 6.86 us
  waiting for transfers between devices: 7.34 us -> 10.5 us
  local copies, waits for them, and re-layouts: 0.97 us -> 0 us
  starting transfers between devices: 14.2 us -> 13.7 us
    pallas_call x3 -> x1, Pallas kernels: 11.7 us -> 5.88 us  [project(): pl.pallas_call(functools.partial(project_kernel, n, sizes), out_shape=tup...]
    ppermute x10, waiting for transfers between devices: 7.34 us -> 10.5 us  [body(): lax.ppermute(x, 'dp', [(i, i ^ (bo if i % 2 else be)) for i in range(n)])]
    unnamed x4 -> x0, local copies, waits for them, and re-layouts: 0.97 us -> none
    ppermute x10, starting transfers between devices: 14.2 us -> 13.7 us  [body(): lax.ppermute(x, 'dp', [(i, i ^ (bo if i % 2 else be)) for i in range(n)])]
  transfers between devices with their start and end apart: 10 -> 10, of which waited for: 5 -> 6; matrix products, arithmetic and copies ran while one was open for 0% -> 0% of each run, Pallas kernels for 24% -> 1%
where the time goes in v3:
time: 31.2 us; the launch traced here: 31.1 us
  starting transfers between devices  13.7 us (44%)
  waiting for transfers between devices  10.5 us (34%)
  Pallas kernels  6.86 us (22%)
    ppermute x10, starting transfers between devices, body(): lax.ppermute(x, 'dp', [(i, i ^ (bo if i % 2 else be)) for i in range(n)])  13.7 us
    ppermute x10, waiting for transfers between devices, body(): lax.ppermute(x, 'dp', [(i, i ^ (bo if i % 2 else be)) for i in range(n)])  10.5 us
    pallas_call x1, Pallas kernels, project(): pl.pallas_call(functools.partial(project_kernel, n, sizes), out_shape=tup...  5.88 us
    pallas_call x1, Pallas kernels, score(): pl.pallas_call(score_kernel, out_shape=jax.ShapeDtypeStruct((arrays[0].sh...  0.81 us
  transfers between devices with their start and end apart: 10, of which 6 were waited for; matrix products, arithmetic and copies ran while one was open for 0% of the time, Pallas kernels for 1%

profile of v3, /device:TPU:0, one launch (start us, length us, event | category | flops | bytes accessed | tf_op | source)
XLA Modules:
  0.0 31.1 jit_solution(14857790307084931590)
XLA Ops:
  0.0 5.9 %project.1 = (f32[10,64,128]{2,1,0:T(8,128)S(1)}, f32[10,64,128]{2,1,0:T(8,128)S(1)}, f32[10,64,128]{2,1,0:T(8,128)S(1)}, f32[10,64,128]{2,1,0:T(8,128)S(1)}) custom-call(bf16[8,2,1,128,512]{4,3,2,1,0:T(8,128)(2,1)} %bitcast.5, bf16[4,128,512]{2,1,0:T(8,128)(2,1)} %bitcast.7, bf16[64,512]{1,0:T(8,128)(2,1)} %refs_2_.1, ...), custom_call_target="tpu_custom_call" | custom-call | flops 754974720 | bytes 11796480 | tf_op jit(solution)/shard_map/project/pallas_call | solution.py:97
  5.9 0.5 %collective-permute-start = (f32[10,64,128]{2,1,0:T(8,128)S(1)}, f32[10,64,128]{2,1,0:T(8,128)S(1)}, u32[]{:S(2)}, u32[]{:S(2)}) collective-permute-start(f32[10,64,128]{2,1,0:T(8,128)S(1)} %get-tuple-element.26), channel_id=1, source_target_pairs={{0,1},{1,0},{2,3},{3,2},{4,5},{5,4},{6,7},{7,6},{8,9},{9,8},{10,11... | collective-permute-start | bytes 983048 | tf_op jit(solution)/shard_map/ppermute | solution.py:187
  6.4 0.1 collective-permute-start.4
  6.5 1.2 %collective-permute-done.got = f32[10,64,128]{2,1,0:T(8,128)S(1)} collective-permute-done((f32[10,64,128]{2,1,0:T(8,128)S(1)}, f32[10,64,128]{2,1,0:T(8,128)S(1)}, u32[]{:S(2)}, u32[]{:S(2)}) %collective-permute-start) | collective-permute-done | bytes 327712 | tf_op jit(solution)/shard_map/ppermute | solution.py:187
  7.7 2.9 %collective-permute-start.1 = (f32[6,64,128]{2,1,0:T(8,128)S(1)}, f32[6,64,128]{2,1,0:T(8,128)S(1)}, u32[]{:S(2)}, u32[]{:S(2)}) collective-permute-start(f32[6,64,128]{2,1,0:T(8,128)S(1)} %get-tuple-element.28.query), channel_id=1, source_target_pairs={{0,2},{1,5},{2,0},{3,7},{4,6},{5,1},{6,4},{7,3},{8,10},{9,13},{10,... | collective-permute-start | bytes 589832 | tf_op jit(solution)/shard_map/ppermute | solution.py:187
  10.7 0.0 collective-permute-done.4.got
  10.7 0.4 %collective-permute-start.5 = (f32[6,64,128]{2,1,0:T(8,128)S(1)}, f32[6,64,128]{2,1,0:T(8,128)S(1)}, u32[]{:S(2)}, u32[]{:S(2)}) collective-permute-start(f32[6,64,128]{2,1,0:T(8,128)S(1)} %get-tuple-element.37.query), channel_id=1, source_target_pairs={{0,2},{1,5},{2,0},{3,7},{4,6},{5,1},{6,4},{7,3},{8,10},{9,13},{10,... | collective-permute-start | bytes 589832 | tf_op jit(solution)/shard_map/ppermute | solution.py:187
  11.1 3.2 %collective-permute-done.1.got = f32[6,64,128]{2,1,0:T(8,128)S(1)} collective-permute-done((f32[6,64,128]{2,1,0:T(8,128)S(1)}, f32[6,64,128]{2,1,0:T(8,128)S(1)}, u32[]{:S(2)}, u32[]{:S(2)}) %collective-permute-start.1) | collective-permute-done | bytes 196640 | tf_op jit(solution)/shard_map/ppermute | solution.py:187
  14.3 2.1 %collective-permute-start.2 = (f32[4,64,128]{2,1,0:T(8,128)S(1)}, f32[4,64,128]{2,1,0:T(8,128)S(1)}, u32[]{:S(2)}, u32[]{:S(2)}) collective-permute-start(f32[4,64,128]{2,1,0:T(8,128)S(1)} %get-tuple-element.30.query), channel_id=1, source_target_pairs={{0,4},{1,9},{2,6},{3,11},{4,0},{5,13},{6,2},{7,15},{8,12},{9,1},{1... | collective-permute-start | bytes 393224 | tf_op jit(solution)/shard_map/ppermute | solution.py:187
  16.5 0.0 collective-permute-done.5.got
  16.5 2.1 %collective-permute-start.6 = (f32[4,64,128]{2,1,0:T(8,128)S(1)}, f32[4,64,128]{2,1,0:T(8,128)S(1)}, u32[]{:S(2)}, u32[]{:S(2)}) collective-permute-start(f32[4,64,128]{2,1,0:T(8,128)S(1)} %get-tuple-element.39.query), channel_id=1, source_target_pairs={{0,4},{1,9},{2,6},{3,11},{4,0},{5,13},{6,2},{7,15},{8,12},{9,1},{1... | collective-permute-start | bytes 393224 | tf_op jit(solution)/shard_map/ppermute | solution.py:187
  18.6 1.7 %collective-permute-done.2.got = f32[4,64,128]{2,1,0:T(8,128)S(1)} collective-permute-done((f32[4,64,128]{2,1,0:T(8,128)S(1)}, f32[4,64,128]{2,1,0:T(8,128)S(1)}, u32[]{:S(2)}, u32[]{:S(2)}) %collective-permute-start.2) | collective-permute-done | bytes 131104 | tf_op jit(solution)/shard_map/ppermute | solution.py:187
  20.3 3.0 %collective-permute-start.3 = (f32[3,64,128]{2,1,0:T(8,128)S(1)}, f32[3,64,128]{2,1,0:T(8,128)S(1)}, u32[]{:S(2)}, u32[]{:S(2)}) collective-permute-start(f32[3,64,128]{2,1,0:T(8,128)S(1)} %get-tuple-element.32.query), channel_id=1, source_target_pairs={{0,8},{1,3},{2,10},{3,1},{4,12},{5,7},{6,14},{7,5},{8,0},{9,11},{1... | collective-permute-start | bytes 294920 | tf_op jit(solution)/shard_map/ppermute | solution.py:187
  23.4 0.0 collective-permute-done.6.got
  23.4 2.3 %collective-permute-start.7 = (f32[3,64,128]{2,1,0:T(8,128)S(1)}, f32[3,64,128]{2,1,0:T(8,128)S(1)}, u32[]{:S(2)}, u32[]{:S(2)}) collective-permute-start(f32[3,64,128]{2,1,0:T(8,128)S(1)} %get-tuple-element.41.query), channel_id=1, source_target_pairs={{0,8},{1,3},{2,10},{3,1},{4,12},{5,7},{6,14},{7,5},{8,0},{9,11},{1... | collective-permute-start | bytes 294920 | tf_op jit(solution)/shard_map/ppermute | solution.py:187
  25.7 0.3 collective-permute-done.3.got
  26.0 0.1 collective-permute-start.8
  26.1 2.9 %collective-permute-done.7.got = f32[3,64,128]{2,1,0:T(8,128)S(1)} collective-permute-done((f32[3,64,128]{2,1,0:T(8,128)S(1)}, f32[3,64,128]{2,1,0:T(8,128)S(1)}, u32[]{:S(2)}, u32[]{:S(2)}) %collective-permute-start.7) | collective-permute-done | bytes 98336 | tf_op jit(solution)/shard_map/ppermute | solution.py:187
  29.0 0.1 collective-permute-start.9
  29.1 0.0 collective-permute-done.8.other_a
  29.1 1.2 %collective-permute-done.9.other_b = bf16[2,64,128]{2,1,0:T(8,128)(2,1)S(1)} collective-permute-done((bf16[2,64,128]{2,1,0:T(8,128)(2,1)S(1)}, bf16[2,64,128]{2,1,0:T(8,128)(2,1)S(1)}, u32[]{:S(2)}, u32[]{:S(2)}) %collective-permute-start.9) | collective-permute-done | bytes 32800 | tf_op jit(solution)/shard_map/ppermute | solution.py:187
  30.3 0.8 %score.1 = f32[1,4]{1,0:T(1,128)} custom-call(bf16[1,64,128]{2,1,0:T(8,128)(2,1)S(1)} %get-tuple-element.33.own_a, bf16[1,64,128]{2,1,0:T(8,128)(2,1)S(1)} %get-tuple-element.42.own_b, bf16[2,64,128]{2,1,0:T(8,128)(2,1)S(1)} %get-tuple-element.43.mine_a, bf16[2,64,128]{2,1,0:T(8,128)(2,1)S(1)} %get-tuple-element.44.mine_b, ...), custom_call_target="tpu_custom_call" | custom-call | tf_op jit(solution)/shard_map/score/pallas_call | solution.py:174
  (8 shorter events, 0.2 us)
Async XLA Ops:
  5.9 1.8 %collective-permute-start = (f32[10,64,128]{2,1,0:T(8,128)S(1)}, f32[10,64,128]{2,1,0:T(8,128)S(1)}, u32[]{:S(2)}, u32[]{:S(2)}) collective-permute-start(f32[10,64,128]{2,1,0:T(8,128)S(1)} %get-tuple-element.26), channel_id=1, source_target_pairs={{0,1},{1,0},{2,3},{3,2},{4,5},{5,4},{6,7},{7,6},{8,9},{9,8},{10,11... | collective-permute-start | bytes 983048 | tf_op jit(solution)/shard_map/ppermute | solution.py:187
  6.4 4.2 %collective-permute-start.4 = (f32[10,64,128]{2,1,0:T(8,128)S(1)}, f32[10,64,128]{2,1,0:T(8,128)S(1)}, u32[]{:S(2)}, u32[]{:S(2)}) collective-permute-start(f32[10,64,128]{2,1,0:T(8,128)S(1)} %get-tuple-element.35), channel_id=1, source_target_pairs={{0,1},{1,0},{2,3},{3,2},{4,5},{5,4},{6,7},{7,6},{8,9},{9,8},{10,11... | collective-permute-start | bytes 983048 | tf_op jit(solution)/shard_map/ppermute | solution.py:187
  7.7 6.6 %collective-permute-start.1 = (f32[6,64,128]{2,1,0:T(8,128)S(1)}, f32[6,64,128]{2,1,0:T(8,128)S(1)}, u32[]{:S(2)}, u32[]{:S(2)}) collective-permute-start(f32[6,64,128]{2,1,0:T(8,128)S(1)} %get-tuple-element.28.query), channel_id=1, source_target_pairs={{0,2},{1,5},{2,0},{3,7},{4,6},{5,1},{6,4},{7,3},{8,10},{9,13},{10,... | collective-permute-start | bytes 589832 | tf_op jit(solution)/shard_map/ppermute | solution.py:187
  10.7 5.8 %collective-permute-start.5 = (f32[6,64,128]{2,1,0:T(8,128)S(1)}, f32[6,64,128]{2,1,0:T(8,128)S(1)}, u32[]{:S(2)}, u32[]{:S(2)}) collective-permute-start(f32[6,64,128]{2,1,0:T(8,128)S(1)} %get-tuple-element.37.query), channel_id=1, source_target_pairs={{0,2},{1,5},{2,0},{3,7},{4,6},{5,1},{6,4},{7,3},{8,10},{9,13},{10,... | collective-permute-start | bytes 589832 | tf_op jit(solution)/shard_map/ppermute | solution.py:187
  14.3 6.0 %collective-permute-start.2 = (f32[4,64,128]{2,1,0:T(8,128)S(1)}, f32[4,64,128]{2,1,0:T(8,128)S(1)}, u32[]{:S(2)}, u32[]{:S(2)}) collective-permute-start(f32[4,64,128]{2,1,0:T(8,128)S(1)} %get-tuple-element.30.query), channel_id=1, source_target_pairs={{0,4},{1,9},{2,6},{3,11},{4,0},{5,13},{6,2},{7,15},{8,12},{9,1},{1... | collective-permute-start | bytes 393224 | tf_op jit(solution)/shard_map/ppermute | solution.py:187
  16.5 6.9 %collective-permute-start.6 = (f32[4,64,128]{2,1,0:T(8,128)S(1)}, f32[4,64,128]{2,1,0:T(8,128)S(1)}, u32[]{:S(2)}, u32[]{:S(2)}) collective-permute-start(f32[4,64,128]{2,1,0:T(8,128)S(1)} %get-tuple-element.39.query), channel_id=1, source_target_pairs={{0,4},{1,9},{2,6},{3,11},{4,0},{5,13},{6,2},{7,15},{8,12},{9,1},{1... | collective-permute-start | bytes 393224 | tf_op jit(solution)/shard_map/ppermute | solution.py:187
  20.3 5.6 %collective-permute-start.3 = (f32[3,64,128]{2,1,0:T(8,128)S(1)}, f32[3,64,128]{2,1,0:T(8,128)S(1)}, u32[]{:S(2)}, u32[]{:S(2)}) collective-permute-start(f32[3,64,128]{2,1,0:T(8,128)S(1)} %get-tuple-element.32.query), channel_id=1, source_target_pairs={{0,8},{1,3},{2,10},{3,1},{4,12},{5,7},{6,14},{7,5},{8,0},{9,11},{1... | collective-permute-start | bytes 294920 | tf_op jit(solution)/shard_map/ppermute | solution.py:187
  23.4 5.6 %collective-permute-start.7 = (f32[3,64,128]{2,1,0:T(8,128)S(1)}, f32[3,64,128]{2,1,0:T(8,128)S(1)}, u32[]{:S(2)}, u32[]{:S(2)}) collective-permute-start(f32[3,64,128]{2,1,0:T(8,128)S(1)} %get-tuple-element.41.query), channel_id=1, source_target_pairs={{0,8},{1,3},{2,10},{3,1},{4,12},{5,7},{6,14},{7,5},{8,0},{9,11},{1... | collective-permute-start | bytes 294920 | tf_op jit(solution)/shard_map/ppermute | solution.py:187
  26.0 3.1 %collective-permute-start.8 = (bf16[2,64,128]{2,1,0:T(8,128)(2,1)S(1)}, bf16[2,64,128]{2,1,0:T(8,128)(2,1)S(1)}, u32[]{:S(2)}, u32[]{:S(2)}) collective-permute-start(bf16[2,64,128]{2,1,0:T(8,128)(2,1)S(1)} %get-tuple-element.43.mine_a), channel_id=1, source_target_pairs={{0,1},{1,0},{2,3},{3,2},{4,5},{5,4},{6,7},{7,6},{8,9},{9,8},{10,11... | collective-permute-start | bytes 98312 | tf_op jit(solution)/shard_map/ppermute | solution.py:187
  29.0 1.3 %collective-permute-start.9 = (bf16[2,64,128]{2,1,0:T(8,128)(2,1)S(1)}, bf16[2,64,128]{2,1,0:T(8,128)(2,1)S(1)}, u32[]{:S(2)}, u32[]{:S(2)}) collective-permute-start(bf16[2,64,128]{2,1,0:T(8,128)(2,1)S(1)} %get-tuple-element.44.mine_b), channel_id=1, source_target_pairs={{0,1},{1,0},{2,3},{3,2},{4,5},{5,4},{6,7},{7,6},{8,9},{9,8},{10,11... | collective-permute-start | bytes 98312 | tf_op jit(solution)/shard_map/ppermute | solution.py:187

commit v4 on v3

--- a/solution.py
+++ b/solution.py
@@ -16,19 +16,17 @@
 
 
 def axis_orders(n):
-    bits = [1 << k for k in range(1, n.bit_length() - 1)]
+    bits = list(range(1, n.bit_length() - 1))
     turn = len(bits) // 2
-    return bits, bits[turn:] + bits[:turn]
+    first, rest = bits[:turn], bits[turn:]
+    return rest[:-1] + first + rest[-1:], first + rest[::-1]
 
 
 def place_of(me, core, pair, n):
     even, odd = axis_orders(n)
-    place = 0
-    for bit_even, bit_odd in zip(even, odd, strict=True):
-        differs = [(me // bit) % 2 != (pair // (bit // 2)) % 2 for bit in (bit_even, bit_odd)]
-        stays = jnp.where(core == 0, jnp.where(differs[0], 0, 1), jnp.where(differs[1], 0, 1))
-        place = 2 * place + stays
-    return place
+    stays = [1 - (((me >> bit) & 1) ^ ((pair >> (bit - 1)) & 1)) for bit in range(1, len(even) + 1)]
+    places = [sum(stays[bit - 1] << (len(order) - 1 - i) for i, bit in enumerate(order)) for order in (even, odd)]
+    return jnp.where(core == 0, *places)
 
 
 def groups(count, size):
@@ -43,7 +41,8 @@
     me = lax.axis_index("dp")
     mine = me % 2
     pending = []
-    for side, (whole, held) in enumerate(zip(sides, buffers, strict=True)):
+    for side in range(2):
+        whole, held = sides[side], buffers[side]
         count = whole[0].shape[0]
         copies = [
             pltpu.make_async_copy(whole[2], held[2], sems.at[side, 0]),
@@ -54,9 +53,10 @@
             copies.append(pltpu.make_async_copy(whole[0].at[pl.ds(at, k)], held[0].at[pl.ds(at, k)], sems.at[side, 2 + j]))
         for copy in copies:
             copy.start()
-        pending.append((copies, spans))
+        pending.append((side, copies, spans))
     places = {}
-    for (copies, spans), (train, query, proj), out in zip(pending, buffers, outs, strict=True):
+    for side, copies, spans in pending:
+        (train, query, proj), out = buffers[side], outs[side]
         count, _, units = train.shape[:3]
         queries = query.shape[0] // 2
         copies[0].wait()
@@ -86,7 +86,7 @@
     views, outs, scratch, flops, moved = [], [], [], 0, 0
     for train, query, proj in sides:
         rank, width = proj.shape
-        views += [pltpu.with_memory_space_constraint(v, pltpu.HBM) for v in (train.reshape(n // 2, 2, -1, SEQ, width), query.reshape(-1, SEQ, width), proj)]
+        views += [train.reshape(n // 2, 2, -1, SEQ, width), query.reshape(-1, SEQ, width), proj]
         units, queries = views[-3].shape[2], views[-2].shape[0] // 2
         outs += [jax.ShapeDtypeStruct((n // 2 * units + queries, rank, SEQ), jnp.float32)] * 2
         scratch += [pltpu.VMEM(view.shape, view.dtype) for view in views[-3:]]
@@ -103,7 +103,7 @@
         compiler_params=LARGE,
         cost_estimate=pl.CostEstimate(flops=flops, bytes_accessed=moved, transcendentals=0),
         name="project",
-    )(*views)
+    )(*[pltpu.with_memory_space_constraint(view, pltpu.HBM) for view in views])
 
 
 def combine_kernel(held, query, got, send, keep):
@@ -184,11 +184,11 @@
 def body(train_inputs, train_grads, query_inputs, query_grads, proj_in, proj_out):
     n = lax.axis_size("dp")
     even, odd = axis_orders(n)
-    swap = lambda x, be, bo: lax.ppermute(x, "dp", [(i, i ^ (bo if i % 2 else be)) for i in range(n)])
+    swap = lambda x, be, bo: lax.ppermute(x, "dp", [(i, i ^ (1 << (bo if i % 2 else be))) for i in range(n)])
     q = query_inputs.shape[0] // SEQ // 2
     sides = ((train_grads, query_grads, proj_out), (train_inputs, query_inputs, proj_in))
     send_a, held_a, send_b, held_b = project(n, (4, 2), *sides)
-    sides = [(held_a, held_a, swap(send_a, 1, 1)), (held_b, held_b, swap(send_b, 1, 1))]
+    sides = [(held_a, held_a, swap(send_a, 0, 0)), (held_b, held_b, swap(send_b, 0, 0))]
     h = held_a.shape[0] - q
     for be, bo in zip(even, odd, strict=True):
         h //= 2
@@ -196,7 +196,7 @@
             query, held = combine(held, query, got, h, q)
             sides[s] = (held, query, swap(query, be, bo))
     (own_a, mine_a), (own_b, mine_b) = [finish(*side) for side in sides]
-    other_a, other_b = swap(mine_a, 1, 1), swap(mine_b, 1, 1)
+    other_a, other_b = swap(mine_a, 0, 0), swap(mine_b, 0, 0)
     return score(own_a, own_b, mine_a, mine_b, other_a, other_b)
 
 

time: 31.2 us -> 30.4 us (0.974)
  waiting for transfers between devices: 10.5 us -> 9.76 us
    ppermute x10, waiting for transfers between devices: 10.5 us -> 9.76 us  [body(): lax.ppermute(x, 'dp', [(i, i ^ 1 << (bo if i % 2 else be)) for i in range...]
  transfers between devices with their start and end apart: 10 -> 10, of which waited for: 6 -> 7; matrix products, arithmetic and copies ran while one was open for 0% -> 0% of each run, Pallas kernels for 1% -> 1%
where the time goes in v4:
time: 30.4 us; the launch traced here: 30.2 us
  starting transfers between devices  13.6 us (45%)
  waiting for transfers between devices  9.76 us (32%)
  Pallas kernels  6.86 us (23%)
    ppermute x10, starting transfers between devices, body(): lax.ppermute(x, 'dp', [(i, i ^ 1 << (bo if i % 2 else be)) for i in range...  13.6 us
    ppermute x10, waiting for transfers between devices, body(): lax.ppermute(x, 'dp', [(i, i ^ 1 << (bo if i % 2 else be)) for i in range...  9.76 us
    pallas_call x1, Pallas kernels, project(): pl.pallas_call(functools.partial(project_kernel, n, sizes), out_shape=tup...  5.88 us
    pallas_call x1, Pallas kernels, score(): pl.pallas_call(score_kernel, out_shape=jax.ShapeDtypeStruct((arrays[0].sh...  0.81 us
  transfers between devices with their start and end apart: 10, of which 7 were waited for; matrix products, arithmetic and copies ran while one was open for 0% of the time, Pallas kernels for 1%

profile of v4, /device:TPU:0, one launch (start us, length us, event | category | flops | bytes accessed | tf_op | source)
XLA Modules:
  0.0 30.2 jit_solution(3819670465971128002)
XLA Ops:
  0.0 5.9 %project.1 = (f32[10,64,128]{2,1,0:T(8,128)S(1)}, f32[10,64,128]{2,1,0:T(8,128)S(1)}, f32[10,64,128]{2,1,0:T(8,128)S(1)}, f32[10,64,128]{2,1,0:T(8,128)S(1)}) custom-call(bf16[8,2,1,128,512]{4,3,2,1,0:T(8,128)(2,1)} %bitcast.5, bf16[4,128,512]{2,1,0:T(8,128)(2,1)} %bitcast.7, bf16[64,512]{1,0:T(8,128)(2,1)} %refs_2_.1, ...), custom_call_target="tpu_custom_call" | custom-call | flops 754974720 | bytes 11796480 | tf_op jit(solution)/shard_map/project/pallas_call | solution.py:97
  5.9 0.5 %collective-permute-start = (f32[10,64,128]{2,1,0:T(8,128)S(1)}, f32[10,64,128]{2,1,0:T(8,128)S(1)}, u32[]{:S(2)}, u32[]{:S(2)}) collective-permute-start(f32[10,64,128]{2,1,0:T(8,128)S(1)} %get-tuple-element.26), channel_id=1, source_target_pairs={{0,1},{1,0},{2,3},{3,2},{4,5},{5,4},{6,7},{7,6},{8,9},{9,8},{10,11... | collective-permute-start | bytes 983048 | tf_op jit(solution)/shard_map/ppermute | solution.py:187
  6.4 0.1 collective-permute-start.4
  6.5 1.2 %collective-permute-done.got = f32[10,64,128]{2,1,0:T(8,128)S(1)} collective-permute-done((f32[10,64,128]{2,1,0:T(8,128)S(1)}, f32[10,64,128]{2,1,0:T(8,128)S(1)}, u32[]{:S(2)}, u32[]{:S(2)}) %collective-permute-start) | collective-permute-done | bytes 327712 | tf_op jit(solution)/shard_map/ppermute | solution.py:187
  7.7 3.0 %collective-permute-start.1 = (f32[6,64,128]{2,1,0:T(8,128)S(1)}, f32[6,64,128]{2,1,0:T(8,128)S(1)}, u32[]{:S(2)}, u32[]{:S(2)}) collective-permute-start(f32[6,64,128]{2,1,0:T(8,128)S(1)} %get-tuple-element.28.query), channel_id=1, source_target_pairs={{0,4},{1,3},{2,6},{3,1},{4,0},{5,7},{6,2},{7,5},{8,12},{9,11},{10,... | collective-permute-start | bytes 589832 | tf_op jit(solution)/shard_map/ppermute | solution.py:187
  10.7 0.0 collective-permute-done.4.got
  10.8 0.4 %collective-permute-start.5 = (f32[6,64,128]{2,1,0:T(8,128)S(1)}, f32[6,64,128]{2,1,0:T(8,128)S(1)}, u32[]{:S(2)}, u32[]{:S(2)}) collective-permute-start(f32[6,64,128]{2,1,0:T(8,128)S(1)} %get-tuple-element.37.query), channel_id=1, source_target_pairs={{0,4},{1,3},{2,6},{3,1},{4,0},{5,7},{6,2},{7,5},{8,12},{9,11},{10,... | collective-permute-start | bytes 589832 | tf_op jit(solution)/shard_map/ppermute | solution.py:187
  11.2 3.2 %collective-permute-done.1.got = f32[6,64,128]{2,1,0:T(8,128)S(1)} collective-permute-done((f32[6,64,128]{2,1,0:T(8,128)S(1)}, f32[6,64,128]{2,1,0:T(8,128)S(1)}, u32[]{:S(2)}, u32[]{:S(2)}) %collective-permute-start.1) | collective-permute-done | bytes 196640 | tf_op jit(solution)/shard_map/ppermute | solution.py:187
  14.4 2.0 %collective-permute-start.2 = (f32[4,64,128]{2,1,0:T(8,128)S(1)}, f32[4,64,128]{2,1,0:T(8,128)S(1)}, u32[]{:S(2)}, u32[]{:S(2)}) collective-permute-start(f32[4,64,128]{2,1,0:T(8,128)S(1)} %get-tuple-element.30.query), channel_id=1, source_target_pairs={{0,2},{1,9},{2,0},{3,11},{4,6},{5,13},{6,4},{7,15},{8,10},{9,1},{1... | collective-permute-start | bytes 393224 | tf_op jit(solution)/shard_map/ppermute | solution.py:187
  16.4 0.1 collective-permute-done.5.got
  16.5 2.0 %collective-permute-start.6 = (f32[4,64,128]{2,1,0:T(8,128)S(1)}, f32[4,64,128]{2,1,0:T(8,128)S(1)}, u32[]{:S(2)}, u32[]{:S(2)}) collective-permute-start(f32[4,64,128]{2,1,0:T(8,128)S(1)} %get-tuple-element.39.query), channel_id=1, source_target_pairs={{0,2},{1,9},{2,0},{3,11},{4,6},{5,13},{6,4},{7,15},{8,10},{9,1},{1... | collective-permute-start | bytes 393224 | tf_op jit(solution)/shard_map/ppermute | solution.py:187
  18.5 0.9 %collective-permute-done.2.got = f32[4,64,128]{2,1,0:T(8,128)S(1)} collective-permute-done((f32[4,64,128]{2,1,0:T(8,128)S(1)}, f32[4,64,128]{2,1,0:T(8,128)S(1)}, u32[]{:S(2)}, u32[]{:S(2)}) %collective-permute-start.2) | collective-permute-done | bytes 131104 | tf_op jit(solution)/shard_map/ppermute | solution.py:187
  19.4 3.1 %collective-permute-start.3 = (f32[3,64,128]{2,1,0:T(8,128)S(1)}, f32[3,64,128]{2,1,0:T(8,128)S(1)}, u32[]{:S(2)}, u32[]{:S(2)}) collective-permute-start(f32[3,64,128]{2,1,0:T(8,128)S(1)} %get-tuple-element.32.query), channel_id=1, source_target_pairs={{0,8},{1,5},{2,10},{3,7},{4,12},{5,1},{6,14},{7,3},{8,0},{9,13},{1... | collective-permute-start | bytes 294920 | tf_op jit(solution)/shard_map/ppermute | solution.py:187
  22.5 0.0 collective-permute-done.6.got
  22.6 2.3 %collective-permute-start.7 = (f32[3,64,128]{2,1,0:T(8,128)S(1)}, f32[3,64,128]{2,1,0:T(8,128)S(1)}, u32[]{:S(2)}, u32[]{:S(2)}) collective-permute-start(f32[3,64,128]{2,1,0:T(8,128)S(1)} %get-tuple-element.41.query), channel_id=1, source_target_pairs={{0,8},{1,5},{2,10},{3,7},{4,12},{5,1},{6,14},{7,3},{8,0},{9,13},{1... | collective-permute-start | bytes 294920 | tf_op jit(solution)/shard_map/ppermute | solution.py:187
  24.8 0.9 %collective-permute-done.3.got = f32[3,64,128]{2,1,0:T(8,128)S(1)} collective-permute-done((f32[3,64,128]{2,1,0:T(8,128)S(1)}, f32[3,64,128]{2,1,0:T(8,128)S(1)}, u32[]{:S(2)}, u32[]{:S(2)}) %collective-permute-start.3) | collective-permute-done | bytes 98336 | tf_op jit(solution)/shard_map/ppermute | solution.py:187
  25.7 0.1 collective-permute-start.8
  25.8 2.3 %collective-permute-done.7.got = f32[3,64,128]{2,1,0:T(8,128)S(1)} collective-permute-done((f32[3,64,128]{2,1,0:T(8,128)S(1)}, f32[3,64,128]{2,1,0:T(8,128)S(1)}, u32[]{:S(2)}, u32[]{:S(2)}) %collective-permute-start.7) | collective-permute-done | bytes 98336 | tf_op jit(solution)/shard_map/ppermute | solution.py:187
  28.2 0.1 collective-permute-start.9
  28.2 0.0 collective-permute-done.8.other_a
  28.2 1.2 %collective-permute-done.9.other_b = bf16[2,64,128]{2,1,0:T(8,128)(2,1)S(1)} collective-permute-done((bf16[2,64,128]{2,1,0:T(8,128)(2,1)S(1)}, bf16[2,64,128]{2,1,0:T(8,128)(2,1)S(1)}, u32[]{:S(2)}, u32[]{:S(2)}) %collective-permute-start.9) | collective-permute-done | bytes 32800 | tf_op jit(solution)/shard_map/ppermute | solution.py:187
  29.4 0.8 %score.1 = f32[1,4]{1,0:T(1,128)} custom-call(bf16[1,64,128]{2,1,0:T(8,128)(2,1)S(1)} %get-tuple-element.33.own_a, bf16[1,64,128]{2,1,0:T(8,128)(2,1)S(1)} %get-tuple-element.42.own_b, bf16[2,64,128]{2,1,0:T(8,128)(2,1)S(1)} %get-tuple-element.43.mine_a, bf16[2,64,128]{2,1,0:T(8,128)(2,1)S(1)} %get-tuple-element.44.mine_b, ...), custom_call_target="tpu_custom_call" | custom-call | tf_op jit(solution)/shard_map/score/pallas_call | solution.py:174
  (8 shorter events, 0.2 us)
Async XLA Ops:
  5.9 1.8 %collective-permute-start = (f32[10,64,128]{2,1,0:T(8,128)S(1)}, f32[10,64,128]{2,1,0:T(8,128)S(1)}, u32[]{:S(2)}, u32[]{:S(2)}) collective-permute-start(f32[10,64,128]{2,1,0:T(8,128)S(1)} %get-tuple-element.26), channel_id=1, source_target_pairs={{0,1},{1,0},{2,3},{3,2},{4,5},{5,4},{6,7},{7,6},{8,9},{9,8},{10,11... | collective-permute-start | bytes 983048 | tf_op jit(solution)/shard_map/ppermute | solution.py:187
  6.4 4.3 %collective-permute-start.4 = (f32[10,64,128]{2,1,0:T(8,128)S(1)}, f32[10,64,128]{2,1,0:T(8,128)S(1)}, u32[]{:S(2)}, u32[]{:S(2)}) collective-permute-start(f32[10,64,128]{2,1,0:T(8,128)S(1)} %get-tuple-element.35), channel_id=1, source_target_pairs={{0,1},{1,0},{2,3},{3,2},{4,5},{5,4},{6,7},{7,6},{8,9},{9,8},{10,11... | collective-permute-start | bytes 983048 | tf_op jit(solution)/shard_map/ppermute | solution.py:187
  7.7 6.7 %collective-permute-start.1 = (f32[6,64,128]{2,1,0:T(8,128)S(1)}, f32[6,64,128]{2,1,0:T(8,128)S(1)}, u32[]{:S(2)}, u32[]{:S(2)}) collective-permute-start(f32[6,64,128]{2,1,0:T(8,128)S(1)} %get-tuple-element.28.query), channel_id=1, source_target_pairs={{0,4},{1,3},{2,6},{3,1},{4,0},{5,7},{6,2},{7,5},{8,12},{9,11},{10,... | collective-permute-start | bytes 589832 | tf_op jit(solution)/shard_map/ppermute | solution.py:187
  10.8 5.7 %collective-permute-start.5 = (f32[6,64,128]{2,1,0:T(8,128)S(1)}, f32[6,64,128]{2,1,0:T(8,128)S(1)}, u32[]{:S(2)}, u32[]{:S(2)}) collective-permute-start(f32[6,64,128]{2,1,0:T(8,128)S(1)} %get-tuple-element.37.query), channel_id=1, source_target_pairs={{0,4},{1,3},{2,6},{3,1},{4,0},{5,7},{6,2},{7,5},{8,12},{9,11},{10,... | collective-permute-start | bytes 589832 | tf_op jit(solution)/shard_map/ppermute | solution.py:187
  14.4 5.0 %collective-permute-start.2 = (f32[4,64,128]{2,1,0:T(8,128)S(1)}, f32[4,64,128]{2,1,0:T(8,128)S(1)}, u32[]{:S(2)}, u32[]{:S(2)}) collective-permute-start(f32[4,64,128]{2,1,0:T(8,128)S(1)} %get-tuple-element.30.query), channel_id=1, source_target_pairs={{0,2},{1,9},{2,0},{3,11},{4,6},{5,13},{6,4},{7,15},{8,10},{9,1},{1... | collective-permute-start | bytes 393224 | tf_op jit(solution)/shard_map/ppermute | solution.py:187
  16.5 6.0 %collective-permute-start.6 = (f32[4,64,128]{2,1,0:T(8,128)S(1)}, f32[4,64,128]{2,1,0:T(8,128)S(1)}, u32[]{:S(2)}, u32[]{:S(2)}) collective-permute-start(f32[4,64,128]{2,1,0:T(8,128)S(1)} %get-tuple-element.39.query), channel_id=1, source_target_pairs={{0,2},{1,9},{2,0},{3,11},{4,6},{5,13},{6,4},{7,15},{8,10},{9,1},{1... | collective-permute-start | bytes 393224 | tf_op jit(solution)/shard_map/ppermute | solution.py:187
  19.4 6.3 %collective-permute-start.3 = (f32[3,64,128]{2,1,0:T(8,128)S(1)}, f32[3,64,128]{2,1,0:T(8,128)S(1)}, u32[]{:S(2)}, u32[]{:S(2)}) collective-permute-start(f32[3,64,128]{2,1,0:T(8,128)S(1)} %get-tuple-element.32.query), channel_id=1, source_target_pairs={{0,8},{1,5},{2,10},{3,7},{4,12},{5,1},{6,14},{7,3},{8,0},{9,13},{1... | collective-permute-start | bytes 294920 | tf_op jit(solution)/shard_map/ppermute | solution.py:187
  22.6 5.6 %collective-permute-start.7 = (f32[3,64,128]{2,1,0:T(8,128)S(1)}, f32[3,64,128]{2,1,0:T(8,128)S(1)}, u32[]{:S(2)}, u32[]{:S(2)}) collective-permute-start(f32[3,64,128]{2,1,0:T(8,128)S(1)} %get-tuple-element.41.query), channel_id=1, source_target_pairs={{0,8},{1,5},{2,10},{3,7},{4,12},{5,1},{6,14},{7,3},{8,0},{9,13},{1... | collective-permute-start | bytes 294920 | tf_op jit(solution)/shard_map/ppermute | solution.py:187
  25.7 2.5 %collective-permute-start.8 = (bf16[2,64,128]{2,1,0:T(8,128)(2,1)S(1)}, bf16[2,64,128]{2,1,0:T(8,128)(2,1)S(1)}, u32[]{:S(2)}, u32[]{:S(2)}) collective-permute-start(bf16[2,64,128]{2,1,0:T(8,128)(2,1)S(1)} %get-tuple-element.43.mine_a), channel_id=1, source_target_pairs={{0,1},{1,0},{2,3},{3,2},{4,5},{5,4},{6,7},{7,6},{8,9},{9,8},{10,11... | collective-permute-start | bytes 98312 | tf_op jit(solution)/shard_map/ppermute | solution.py:187
  28.2 1.3 %collective-permute-start.9 = (bf16[2,64,128]{2,1,0:T(8,128)(2,1)S(1)}, bf16[2,64,128]{2,1,0:T(8,128)(2,1)S(1)}, u32[]{:S(2)}, u32[]{:S(2)}) collective-permute-start(bf16[2,64,128]{2,1,0:T(8,128)(2,1)S(1)} %get-tuple-element.44.mine_b), channel_id=1, source_target_pairs={{0,1},{1,0},{2,3},{3,2},{4,5},{5,4},{6,7},{7,6},{8,9},{9,8},{10,11... | collective-permute-start | bytes 98312 | tf_op jit(solution)/shard_map/ppermute | solution.py:187

commit v5 on v4

v5 whole, which is shorter than its diff:
```python
import functools

import jax
import jax.numpy as jnp
from jax import lax
from jax.experimental import pallas as pl
from jax.experimental.pallas import tpu as pltpu
from jax.sharding import PartitionSpec as P

SEQ = 128
NT = (((1,), (1,)), ((), ()))
VMEM = pl.BlockSpec(memory_space=pltpu.VMEM)
ANY = pl.BlockSpec(memory_space=pl.ANY)
HBM = pl.BlockSpec(memory_space=pltpu.HBM)
PARAMS = pltpu.CompilerParams(vmem_limit_bytes=32 * 2**20)
LARGE = pltpu.CompilerParams(vmem_limit_bytes=40 * 2**20)


def axis_orders(n):
    bits = list(range(1, n.bit_length() - 1))
    turn = len(bits) // 2
    first, rest = bits[:turn], bits[turn:]
    return rest[:-1] + first + rest[-1:], first + rest[::-1]


def place_of(me, core, pair, n):
    even, odd = axis_orders(n)
    stays = [1 - (((me >> bit) & 1) ^ ((pair >> (bit - 1)) & 1)) for bit in range(1, len(even) + 1)]
    places = [sum(stays[bit - 1] << (len(order) - 1 - i) for i, bit in enumerate(order)) for order in (even, odd)]
    return jnp.where(core == 0, *places)


def groups(count, size):
    return [(at, min(size, count - at)) for at in range(0, count, size)]


def dot(proj, rows):
    rows = rows.reshape(-1, rows.shape[-1])
    return lax.dot_general(proj, rows, NT, preferred_element_type=jnp.float32)


def put_train(n, core, at, count, units, part, out):
    me = lax.axis_index("dp")
    for i in range(count):
        place = place_of(me, core, at + i, n) * units
        for u in range(units):
            unit = i * units + u
            out[place + u] = part[:, unit * SEQ : (unit + 1) * SEQ]


def put_query(first, part, out):
    for k in range(out.shape[0] - first):
        out[first + k] = part[:, k * SEQ : (k + 1) * SEQ]


def project_kernel(n, sizes, ta, qa, pa, tb, qb, pb, send_a, held_a, send_b, tb_kept, qb_kept, pb_v, ta_v, qa_v, pa_v, tb_v, qb_v, sems):
    mine = lax.axis_index("dp") & 1
    count, _, units = ta.shape[:3]
    queries = qa.shape[0] // 2
    cores = (1 - mine, mine)
    share = lambda core: pl.ds(core * queries, queries)
    spans_a, spans_b = groups(count, sizes[0]), groups(count, sizes[1])
    span = lambda s: pl.ds(s[0], s[1])
    moves = [(pa, pa_v), (qa, qa_v), *((ta.at[span(s)], ta_v.at[span(s)]) for s in spans_a)]
    moves += [(pb, pb_v), (qb.at[share(1 - mine)], qb_v)]
    moves += [(tb.at[span(s), 1 - mine], tb_v.at[span(s)]) for s in spans_b]
    moves += [(qb.at[share(mine)], qb_kept), (tb.at[:, mine], tb_kept)]
    copies = [pltpu.make_async_copy(source, target, sems.at[i]) for i, (source, target) in enumerate(moves)]
    for copy in copies:
        copy.start()
    arrivals = iter(copies)
    next(arrivals).wait()
    next(arrivals).wait()
    outs = (send_a, held_a)
    for core, out in zip(cores, outs, strict=True):
        put_query(count * units, dot(pa_v[...], qa_v[share(core)]), out)
    for at, k in spans_a:
        next(arrivals).wait()
        for core, out in zip(cores, outs, strict=True):
            put_train(n, core, at, k, units, dot(pa_v[...], ta_v[pl.ds(at, k), core]), out)
    next(arrivals).wait()
    next(arrivals).wait()
    put_query(count * units, dot(pb_v[...], qb_v[...]), send_b)
    for at, k in spans_b:
        next(arrivals).wait()
        put_train(n, 1 - mine, at, k, units, dot(pb_v[...], tb_v[pl.ds(at, k)]), send_b)
    for copy in arrivals:
        copy.wait()


def project(n, sizes, *sides):
    views = []
    for train, query, proj in sides:
        views += [train.reshape(n // 2, 2, -1, SEQ, train.shape[1]), query.reshape(-1, SEQ, query.shape[1]), proj]
    count, _, units = views[0].shape[:3]
    queries = views[1].shape[0] // 2
    rank = views[2].shape[0]
    out = jax.ShapeDtypeStruct((count * units + queries, rank, SEQ), jnp.float32)
    tb, qb, pb = views[3:]
    half_train, half_query = (count,) + tb.shape[2:], (queries,) + qb.shape[1:]
    like = lambda shape: jax.ShapeDtypeStruct(shape, tb.dtype)
    copies = 8 - 2 + sum(len(groups(count, size)) for size in sizes)
    rows = (count * units + queries) * SEQ
    return pl.pallas_call(
        functools.partial(project_kernel, n, sizes),
        out_shape=(out, out, out, like(half_train), like(half_query), like(pb.shape)),
        in_specs=[HBM] * 6,
        out_specs=(VMEM,) * 6,
        scratch_shapes=[
            *(pltpu.VMEM(view.shape, view.dtype) for view in views[:3]),
            pltpu.VMEM(half_train, tb.dtype),
            pltpu.VMEM(half_query, qb.dtype),
            pltpu.SemaphoreType.DMA((copies,)),
        ],
        compiler_params=LARGE,
        cost_estimate=pl.CostEstimate(
            flops=2 * rows * rank * (2 * views[2].shape[1] + pb.shape[1]),
            bytes_accessed=4 * rows * (views[2].shape[1] + pb.shape[1]),
            transcendentals=0,
        ),
        name="project",
    )(*[pltpu.with_memory_space_constraint(view, pltpu.HBM) for view in views])


def project_kept_kernel(n, size, train, query, proj, out):
    mine = lax.axis_index("dp") & 1
    count, units = train.shape[:2]
    put_query(count * units, dot(proj[...], query[...]), out)
    for at, k in groups(count, size):
        put_train(n, mine, at, k, units, dot(proj[...], train[pl.ds(at, k)]), out)


def project_kept(n, size, train, query, proj):
    rank, width = proj.shape
    total = train.shape[0] * train.shape[1] + query.shape[0]
    return pl.pallas_call(
        functools.partial(project_kept_kernel, n, size),
        out_shape=jax.ShapeDtypeStruct((total, rank, SEQ), jnp.float32),
        in_specs=[VMEM] * 3,
        out_specs=VMEM,
        compiler_params=PARAMS,
        cost_estimate=pl.CostEstimate(flops=2 * total * SEQ * rank * width, bytes_accessed=2 * total * SEQ * width, transcendentals=0),
        name="project_kept",
    )(train, query, proj)


def combine_kernel(held, query, got, *refs):
    send, keep = refs[-2:]
    h = keep.shape[0]
    q = send.shape[0] - h
    send[pl.ds(0, h)] = held[pl.ds(0, h)] + got[pl.ds(0, h)]
    keep[...] = held[pl.ds(h, h)] + got[pl.ds(h, h)]
    send[pl.ds(h, q)] = query[pl.ds(query.shape[0] - q, q)] + got[pl.ds(2 * h, q)]


def combine(held, query, got, h, q, *earlier):
    tile = got.shape[1:]
    return pl.pallas_call(
        combine_kernel,
        out_shape=(jax.ShapeDtypeStruct((h + q,) + tile, jnp.float32), jax.ShapeDtypeStruct((h,) + tile, jnp.float32)),
        in_specs=[VMEM] * 3 + [ANY] * len(earlier),
        out_specs=(VMEM, VMEM),
        compiler_params=PARAMS,
        name="combine",
    )(held, query, got, *earlier)


def finish_kernel(keep, query, got, own, own_query):
    h = keep.shape[0]
    q = own_query.shape[0]
    own[...] = (keep[...] + got[pl.ds(0, h)]).astype(jnp.bfloat16)
    own_query[...] = (query[pl.ds(h, q)] + got[pl.ds(h, q)]).astype(jnp.bfloat16)


def finish(keep, query, got):
    tile = got.shape[1:]
    h = keep.shape[0]
    return pl.pallas_call(
        finish_kernel,
        out_shape=(
            jax.ShapeDtypeStruct((h,) + tile, jnp.bfloat16),
            jax.ShapeDtypeStruct((query.shape[0] - h,) + tile, jnp.bfloat16),
        ),
        in_specs=[VMEM] * 3,
        out_specs=(VMEM, VMEM),
        compiler_params=PARAMS,
        name="finish",
    )(keep, query, got)


def score_kernel(own_a, own_b, mine_a, mine_b, other_a, other_b, scores):
    core = lax.axis_index("dp") % 2
    count = mine_a.shape[0]
    scale = 1.0 / (SEQ * own_a.shape[1])

    def outer(a, b, k):
        return lax.dot_general(a[k], b[k], NT, preferred_element_type=jnp.float32)

    lane = lax.broadcasted_iota(jnp.int32, scores.shape, 1)
    row = lax.broadcasted_iota(jnp.int32, scores.shape, 0)
    result = jnp.zeros(scores.shape, jnp.float32)
    examples = [outer(own_a, own_b, e) for e in range(scores.shape[0])]
    for a, b, side in ((mine_a, mine_b, core), (other_a, other_b, 1 - core)):
        for k in range(count):
            grad = outer(a, b, k)
            for e, example in enumerate(examples):
                value = jnp.sum(example * grad) * scale
                result = jnp.where((lane == side * count + k) & (row == e), value, result)
    scores[...] = result


def score(*arrays):
    return pl.pallas_call(
        score_kernel,
        out_shape=jax.ShapeDtypeStruct((arrays[0].shape[0], 2 * arrays[2].shape[0]), jnp.float32),
        in_specs=[VMEM] * 6,
        out_specs=VMEM,
        compiler_params=PARAMS,
        name="score",
    )(*arrays)


def body(train_inputs, train_grads, query_inputs, query_grads, proj_in, proj_out):
    n = lax.axis_size("dp")
    even, odd = axis_orders(n)
    swap = lambda x, be, bo: lax.ppermute(x, "dp", [(i, i ^ (1 << (bo if i % 2 else be))) for i in range(n)])
    q = query_inputs.shape[0] // SEQ // 2
    sides = ((train_grads, query_grads, proj_out), (train_inputs, query_inputs, proj_in))
    send_a, held_a, send_b, *kept = project(n, (4, 4), *sides)
    got_a, got_b = swap(send_a, 0, 0), swap(send_b, 0, 0)
    held_b = project_kept(n, 4, *kept)
    sides = [(held_a, held_a, got_a), (held_b, held_b, got_b)]
    earlier = (held_b,)
    h = held_a.shape[0] - q
    for be, bo in zip(even, odd, strict=True):
        h //= 2
        for s, (held, query, got) in enumerate(sides):
            query, held = combine(held, query, got, h, q, *earlier)
            earlier = ()
            sides[s] = (held, query, swap(query, be, bo))
    (own_a, mine_a), (own_b, mine_b) = [finish(*side) for side in sides]
    other_a, other_b = swap(mine_a, 0, 0), swap(mine_b, 0, 0)
    return score(own_a, own_b, mine_a, mine_b, other_a, other_b)


def solution(mesh):
    return jax.shard_map(
        body,
        mesh=mesh,
        in_specs=(
            P("groups", "dp"),
            P("groups", "dp"),
            P("groups", "dp"),
            P("groups", "dp"),
            P(None, "dp"),
            P(None, "dp"),
        ),
        out_specs=P(("groups", "dp"), None),
        check_vma=False,
    )
```

time: 30.4 us -> 29.6 us (0.974)
  waiting for transfers between devices: 9.76 us -> 8.87 us
    ppermute x10, waiting for transfers between devices: 9.76 us -> 8.87 us  [body(): lax.ppermute(x, 'dp', [(i, i ^ 1 << (bo if i % 2 else be)) for i in range...]
    pallas_call x1 -> x2, Pallas kernels: 5.88 us -> 6.14 us  [the longest x1 4.64 us: project(): pl.pallas_call(functools.partial(project_kernel, n, sizes), out_shape=(ou...]
  transfers between devices with their start and end apart: 10 -> 10, of which waited for: 7 -> 6; matrix products, arithmetic and copies ran while one was open for 0% -> 0% of each run, Pallas kernels for 1% -> 6%
where the time goes in v5:
time: 29.6 us; the launch traced here: 29.4 us
  starting transfers between devices  13.4 us (45%)
  waiting for transfers between devices  8.87 us (30%)
  Pallas kernels  7.12 us (24%)
    ppermute x10, starting transfers between devices, body(): lax.ppermute(x, 'dp', [(i, i ^ 1 << (bo if i % 2 else be)) for i in range...  13.4 us
    ppermute x10, waiting for transfers between devices, body(): lax.ppermute(x, 'dp', [(i, i ^ 1 << (bo if i % 2 else be)) for i in range...  8.87 us
    pallas_call x1, Pallas kernels, project(): pl.pallas_call(functools.partial(project_kernel, n, sizes), out_shape=(ou...  4.64 us
    pallas_call x1, Pallas kernels, project_kept(): pl.pallas_call(functools.partial(project_kept_kernel, n, size), out_shape...  1.5 us
    pallas_call x1, Pallas kernels, score(): pl.pallas_call(score_kernel, out_shape=jax.ShapeDtypeStruct((arrays[0].sh...  0.81 us
  transfers between devices with their start and end apart: 10, of which 6 were waited for; matrix products, arithmetic and copies ran while one was open for 0% of the time, Pallas kernels for 6%

profile of v5, /device:TPU:0, one launch (start us, length us, event | category | flops | bytes accessed | tf_op | source)
XLA Modules:
  0.0 29.4 jit_solution(8094994595384508218)
XLA Ops:
  0.0 4.6 %project.1 = (f32[10,64,128]{2,1,0:T(8,128)S(1)}, f32[10,64,128]{2,1,0:T(8,128)S(1)}, f32[10,64,128]{2,1,0:T(8,128)S(1)}, bf16[8,1,128,1792]{3,2,1,0:T(8,128)(2,...) custom-call(bf16[8,2,1,128,512]{4,3,2,1,0:T(8,128)(2,1)} %bitcast.5, ...), custom_call_target="tpu_custom_call" | custom-call | flops 461373440 | bytes 11796480 | tf_op jit(solution)/shard_map/project/pallas_call | solution.py:104
  4.6 0.5 %collective-permute-start = (f32[10,64,128]{2,1,0:T(8,128)S(1)}, f32[10,64,128]{2,1,0:T(8,128)S(1)}, u32[]{:S(2)}, u32[]{:S(2)}) collective-permute-start(f32[10,64,128]{2,1,0:T(8,128)S(1)} %get-tuple-element.28), channel_id=1, source_target_pairs={{0,1},{1,0},{2,3},{3,2},{4,5},{5,4},{6,7},{7,6},{8,9},{9,8},{10,11... | collective-permute-start | bytes 983048 | tf_op jit(solution)/shard_map/ppermute | solution.py:226
  5.2 0.1 collective-permute-start.4
  5.2 1.5 %project_kept.1.refs_0_.held.query = f32[10,64,128]{2,1,0:T(8,128)S(1)} custom-call(bf16[8,1,128,1792]{3,2,1,0:T(8,128)(2,1)S(1)} %get-tuple-element.29.train, bf16[2,128,1792]{2,1,0:T(8,128)(2,1)S(1)} %get-tuple-element.30.query, bf16[64,1792]{1,0:T(8,128)(2,1)S(1)} %get-tuple-element.31.proj), custom_call_target="tpu_custom_call" | custom-call | flops 293601280 | bytes 4587520 | tf_op jit(solution)/shard_map/project_kept/pallas_call | solution.py:136
  6.7 0.0 collective-permute-done.got
  6.8 3.1 %collective-permute-start.1 = (f32[6,64,128]{2,1,0:T(8,128)S(1)}, f32[6,64,128]{2,1,0:T(8,128)S(1)}, u32[]{:S(2)}, u32[]{:S(2)}) collective-permute-start(f32[6,64,128]{2,1,0:T(8,128)S(1)} %get-tuple-element.33.query), channel_id=1, source_target_pairs={{0,4},{1,3},{2,6},{3,1},{4,0},{5,7},{6,2},{7,5},{8,12},{9,11},{10,... | collective-permute-start | bytes 589832 | tf_op jit(solution)/shard_map/ppermute | solution.py:226
  9.9 0.0 collective-permute-done.4.got
  9.9 0.1 collective-permute-start.5
  10.0 3.5 %collective-permute-done.1.got = f32[6,64,128]{2,1,0:T(8,128)S(1)} collective-permute-done((f32[6,64,128]{2,1,0:T(8,128)S(1)}, f32[6,64,128]{2,1,0:T(8,128)S(1)}, u32[]{:S(2)}, u32[]{:S(2)}) %collective-permute-start.1) | collective-permute-done | bytes 196640 | tf_op jit(solution)/shard_map/ppermute | solution.py:226
  13.6 2.0 %collective-permute-start.2 = (f32[4,64,128]{2,1,0:T(8,128)S(1)}, f32[4,64,128]{2,1,0:T(8,128)S(1)}, u32[]{:S(2)}, u32[]{:S(2)}) collective-permute-start(f32[4,64,128]{2,1,0:T(8,128)S(1)} %get-tuple-element.35.query), channel_id=1, source_target_pairs={{0,2},{1,9},{2,0},{3,11},{4,6},{5,13},{6,4},{7,15},{8,10},{9,1},{1... | collective-permute-start | bytes 393224 | tf_op jit(solution)/shard_map/ppermute | solution.py:226
  15.6 0.1 collective-permute-done.5.got
  15.7 2.0 %collective-permute-start.6 = (f32[4,64,128]{2,1,0:T(8,128)S(1)}, f32[4,64,128]{2,1,0:T(8,128)S(1)}, u32[]{:S(2)}, u32[]{:S(2)}) collective-permute-start(f32[4,64,128]{2,1,0:T(8,128)S(1)} %get-tuple-element.43.query), channel_id=1, source_target_pairs={{0,2},{1,9},{2,0},{3,11},{4,6},{5,13},{6,4},{7,15},{8,10},{9,1},{1... | collective-permute-start | bytes 393224 | tf_op jit(solution)/shard_map/ppermute | solution.py:226
  17.7 0.9 %collective-permute-done.2.got = f32[4,64,128]{2,1,0:T(8,128)S(1)} collective-permute-done((f32[4,64,128]{2,1,0:T(8,128)S(1)}, f32[4,64,128]{2,1,0:T(8,128)S(1)}, u32[]{:S(2)}, u32[]{:S(2)}) %collective-permute-start.2) | collective-permute-done | bytes 131104 | tf_op jit(solution)/shard_map/ppermute | solution.py:226
  18.6 3.1 %collective-permute-start.3 = (f32[3,64,128]{2,1,0:T(8,128)S(1)}, f32[3,64,128]{2,1,0:T(8,128)S(1)}, u32[]{:S(2)}, u32[]{:S(2)}) collective-permute-start(f32[3,64,128]{2,1,0:T(8,128)S(1)} %get-tuple-element.37.query), channel_id=1, source_target_pairs={{0,8},{1,5},{2,10},{3,7},{4,12},{5,1},{6,14},{7,3},{8,0},{9,13},{1... | collective-permute-start | bytes 294920 | tf_op jit(solution)/shard_map/ppermute | solution.py:226
  21.7 0.0 collective-permute-done.6.got
  21.7 2.3 %collective-permute-start.7 = (f32[3,64,128]{2,1,0:T(8,128)S(1)}, f32[3,64,128]{2,1,0:T(8,128)S(1)}, u32[]{:S(2)}, u32[]{:S(2)}) collective-permute-start(f32[3,64,128]{2,1,0:T(8,128)S(1)} %get-tuple-element.45.query), channel_id=1, source_target_pairs={{0,8},{1,5},{2,10},{3,7},{4,12},{5,1},{6,14},{7,3},{8,0},{9,13},{1... | collective-permute-start | bytes 294920 | tf_op jit(solution)/shard_map/ppermute | solution.py:226
  24.1 0.8 %collective-permute-done.3.got = f32[3,64,128]{2,1,0:T(8,128)S(1)} collective-permute-done((f32[3,64,128]{2,1,0:T(8,128)S(1)}, f32[3,64,128]{2,1,0:T(8,128)S(1)}, u32[]{:S(2)}, u32[]{:S(2)}) %collective-permute-start.3) | collective-permute-done | bytes 98336 | tf_op jit(solution)/shard_map/ppermute | solution.py:226
  24.9 0.1 collective-permute-start.8
  24.9 2.4 %collective-permute-done.7.got = f32[3,64,128]{2,1,0:T(8,128)S(1)} collective-permute-done((f32[3,64,128]{2,1,0:T(8,128)S(1)}, f32[3,64,128]{2,1,0:T(8,128)S(1)}, u32[]{:S(2)}, u32[]{:S(2)}) %collective-permute-start.7) | collective-permute-done | bytes 98336 | tf_op jit(solution)/shard_map/ppermute | solution.py:226
  27.3 0.1 collective-permute-start.9
  27.4 0.0 collective-permute-done.8.other_a
  27.4 1.2 %collective-permute-done.9.other_b = bf16[2,64,128]{2,1,0:T(8,128)(2,1)S(1)} collective-permute-done((bf16[2,64,128]{2,1,0:T(8,128)(2,1)S(1)}, bf16[2,64,128]{2,1,0:T(8,128)(2,1)S(1)}, u32[]{:S(2)}, u32[]{:S(2)}) %collective-permute-start.9) | collective-permute-done | bytes 32800 | tf_op jit(solution)/shard_map/ppermute | solution.py:226
  28.6 0.8 %score.1 = f32[1,4]{1,0:T(1,128)} custom-call(bf16[1,64,128]{2,1,0:T(8,128)(2,1)S(1)} %get-tuple-element.38.own_a, bf16[1,64,128]{2,1,0:T(8,128)(2,1)S(1)} %get-tuple-element.46.own_b, bf16[2,64,128]{2,1,0:T(8,128)(2,1)S(1)} %get-tuple-element.47.mine_a, bf16[2,64,128]{2,1,0:T(8,128)(2,1)S(1)} %get-tuple-element.48.mine_b, ...), custom_call_target="tpu_custom_call" | custom-call | tf_op jit(solution)/shard_map/score/pallas_call | solution.py:213
  (8 shorter events, 0.2 us)
Async XLA Ops:
  4.6 2.1 %collective-permute-start = (f32[10,64,128]{2,1,0:T(8,128)S(1)}, f32[10,64,128]{2,1,0:T(8,128)S(1)}, u32[]{:S(2)}, u32[]{:S(2)}) collective-permute-start(f32[10,64,128]{2,1,0:T(8,128)S(1)} %get-tuple-element.28), channel_id=1, source_target_pairs={{0,1},{1,0},{2,3},{3,2},{4,5},{5,4},{6,7},{7,6},{8,9},{9,8},{10,11... | collective-permute-start | bytes 983048 | tf_op jit(solution)/shard_map/ppermute | solution.py:226
  5.2 4.7 %collective-permute-start.4 = (f32[10,64,128]{2,1,0:T(8,128)S(1)}, f32[10,64,128]{2,1,0:T(8,128)S(1)}, u32[]{:S(2)}, u32[]{:S(2)}) collective-permute-start(f32[10,64,128]{2,1,0:T(8,128)S(1)} %get-tuple-element.39), channel_id=1, source_target_pairs={{0,1},{1,0},{2,3},{3,2},{4,5},{5,4},{6,7},{7,6},{8,9},{9,8},{10,11... | collective-permute-start | bytes 983048 | tf_op jit(solution)/shard_map/ppermute | solution.py:226
  6.8 6.7 %collective-permute-start.1 = (f32[6,64,128]{2,1,0:T(8,128)S(1)}, f32[6,64,128]{2,1,0:T(8,128)S(1)}, u32[]{:S(2)}, u32[]{:S(2)}) collective-permute-start(f32[6,64,128]{2,1,0:T(8,128)S(1)} %get-tuple-element.33.query), channel_id=1, source_target_pairs={{0,4},{1,3},{2,6},{3,1},{4,0},{5,7},{6,2},{7,5},{8,12},{9,11},{10,... | collective-permute-start | bytes 589832 | tf_op jit(solution)/shard_map/ppermute | solution.py:226
  9.9 5.7 %collective-permute-start.5 = (f32[6,64,128]{2,1,0:T(8,128)S(1)}, f32[6,64,128]{2,1,0:T(8,128)S(1)}, u32[]{:S(2)}, u32[]{:S(2)}) collective-permute-start(f32[6,64,128]{2,1,0:T(8,128)S(1)} %get-tuple-element.41.query), channel_id=1, source_target_pairs={{0,4},{1,3},{2,6},{3,1},{4,0},{5,7},{6,2},{7,5},{8,12},{9,11},{10,... | collective-permute-start | bytes 589832 | tf_op jit(solution)/shard_map/ppermute | solution.py:226
  13.6 5.0 %collective-permute-start.2 = (f32[4,64,128]{2,1,0:T(8,128)S(1)}, f32[4,64,128]{2,1,0:T(8,128)S(1)}, u32[]{:S(2)}, u32[]{:S(2)}) collective-permute-start(f32[4,64,128]{2,1,0:T(8,128)S(1)} %get-tuple-element.35.query), channel_id=1, source_target_pairs={{0,2},{1,9},{2,0},{3,11},{4,6},{5,13},{6,4},{7,15},{8,10},{9,1},{1... | collective-permute-start | bytes 393224 | tf_op jit(solution)/shard_map/ppermute | solution.py:226
  15.7 6.0 %collective-permute-start.6 = (f32[4,64,128]{2,1,0:T(8,128)S(1)}, f32[4,64,128]{2,1,0:T(8,128)S(1)}, u32[]{:S(2)}, u32[]{:S(2)}) collective-permute-start(f32[4,64,128]{2,1,0:T(8,128)S(1)} %get-tuple-element.43.query), channel_id=1, source_target_pairs={{0,2},{1,9},{2,0},{3,11},{4,6},{5,13},{6,4},{7,15},{8,10},{9,1},{1... | collective-permute-start | bytes 393224 | tf_op jit(solution)/shard_map/ppermute | solution.py:226
  18.6 6.2 %collective-permute-start.3 = (f32[3,64,128]{2,1,0:T(8,128)S(1)}, f32[3,64,128]{2,1,0:T(8,128)S(1)}, u32[]{:S(2)}, u32[]{:S(2)}) collective-permute-start(f32[3,64,128]{2,1,0:T(8,128)S(1)} %get-tuple-element.37.query), channel_id=1, source_target_pairs={{0,8},{1,5},{2,10},{3,7},{4,12},{5,1},{6,14},{7,3},{8,0},{9,13},{1... | collective-permute-start | bytes 294920 | tf_op jit(solution)/shard_map/ppermute | solution.py:226
  21.7 5.6 %collective-permute-start.7 = (f32[3,64,128]{2,1,0:T(8,128)S(1)}, f32[3,64,128]{2,1,0:T(8,128)S(1)}, u32[]{:S(2)}, u32[]{:S(2)}) collective-permute-start(f32[3,64,128]{2,1,0:T(8,128)S(1)} %get-tuple-element.45.query), channel_id=1, source_target_pairs={{0,8},{1,5},{2,10},{3,7},{4,12},{5,1},{6,14},{7,3},{8,0},{9,13},{1... | collective-permute-start | bytes 294920 | tf_op jit(solution)/shard_map/ppermute | solution.py:226
  24.9 2.6 %collective-permute-start.8 = (bf16[2,64,128]{2,1,0:T(8,128)(2,1)S(1)}, bf16[2,64,128]{2,1,0:T(8,128)(2,1)S(1)}, u32[]{:S(2)}, u32[]{:S(2)}) collective-permute-start(bf16[2,64,128]{2,1,0:T(8,128)(2,1)S(1)} %get-tuple-element.47.mine_a), channel_id=1, source_target_pairs={{0,1},{1,0},{2,3},{3,2},{4,5},{5,4},{6,7},{7,6},{8,9},{9,8},{10,11... | collective-permute-start | bytes 98312 | tf_op jit(solution)/shard_map/ppermute | solution.py:226
  27.3 1.3 %collective-permute-start.9 = (bf16[2,64,128]{2,1,0:T(8,128)(2,1)S(1)}, bf16[2,64,128]{2,1,0:T(8,128)(2,1)S(1)}, u32[]{:S(2)}, u32[]{:S(2)}) collective-permute-start(bf16[2,64,128]{2,1,0:T(8,128)(2,1)S(1)} %get-tuple-element.48.mine_b), channel_id=1, source_target_pairs={{0,1},{1,0},{2,3},{3,2},{4,5},{5,4},{6,7},{7,6},{8,9},{9,8},{10,11... | collective-permute-start | bytes 98312 | tf_op jit(solution)/shard_map/ppermute | solution.py:226

commit v6 on v5

--- a/solution.py
+++ b/solution.py
@@ -24,10 +24,14 @@
 
 
 def place_of(me, core, pair, n):
-    even, odd = axis_orders(n)
-    stays = [1 - (((me >> bit) & 1) ^ ((pair >> (bit - 1)) & 1)) for bit in range(1, len(even) + 1)]
-    places = [sum(stays[bit - 1] << (len(order) - 1 - i) for i, bit in enumerate(order)) for order in (even, odd)]
-    return jnp.where(core == 0, *places)
+    orders = axis_orders(n)
+
+    def spread(bit_at):
+        return [sum(bit_at(bit) << (len(order) - 1 - i) for i, bit in enumerate(order)) for order in orders]
+
+    own = jnp.where(core == 0, *spread(lambda bit: 1 - ((me >> bit) & 1)))
+    even, odd = spread(lambda bit: (pair >> (bit - 1)) & 1)
+    return own ^ (even if even == odd else jnp.where(core == 0, even, odd))
 
 
 def groups(count, size):
@@ -204,7 +208,8 @@
         for k in range(count):
             grad = outer(a, b, k)
             for e, example in enumerate(examples):
-                value = jnp.sum(example * grad) * scale
+                column = jnp.sum(example * grad, axis=0, keepdims=True)
+                value = jnp.sum(column, axis=1, keepdims=True) * scale
                 result = jnp.where((lane == side * count + k) & (row == e), value, result)
     scores[...] = result
 

time: 29.6 us -> 29.5 us (level)
  no operation moved by 1% of the time
where the time goes in v6:
time: 29.5 us; the launch traced here: 29.4 us
  starting transfers between devices  13.4 us (45%)
  waiting for transfers between devices  8.87 us (30%)
  Pallas kernels  7.08 us (24%)
    ppermute x10, starting transfers between devices, body(): lax.ppermute(x, 'dp', [(i, i ^ 1 << (bo if i % 2 else be)) for i in range...  13.4 us
    ppermute x10, waiting for transfers between devices, body(): lax.ppermute(x, 'dp', [(i, i ^ 1 << (bo if i % 2 else be)) for i in range...  8.87 us
    pallas_call x1, Pallas kernels, project(): pl.pallas_call(functools.partial(project_kernel, n, sizes), out_shape=(ou...  4.64 us
    pallas_call x1, Pallas kernels, project_kept(): pl.pallas_call(functools.partial(project_kept_kernel, n, size), out_shape...  1.5 us
    pallas_call x1, Pallas kernels, score(): pl.pallas_call(score_kernel, out_shape=jax.ShapeDtypeStruct((arrays[0].sh...  0.78 us
  transfers between devices with their start and end apart: 10, of which 6 were waited for; matrix products, arithmetic and copies ran while one was open for 0% of the time, Pallas kernels for 6%

profile of v6, /device:TPU:0, one launch (start us, length us, event | category | flops | bytes accessed | tf_op | source)
XLA Modules:
  0.0 29.4 jit_solution(11140925934529123050)
XLA Ops:
  0.0 4.6 %project.1 = (f32[10,64,128]{2,1,0:T(8,128)S(1)}, f32[10,64,128]{2,1,0:T(8,128)S(1)}, f32[10,64,128]{2,1,0:T(8,128)S(1)}, bf16[8,1,128,1792]{3,2,1,0:T(8,128)(2,...) custom-call(bf16[8,2,1,128,512]{4,3,2,1,0:T(8,128)(2,1)} %bitcast.5, ...), custom_call_target="tpu_custom_call" | custom-call | flops 461373440 | bytes 11796480 | tf_op jit(solution)/shard_map/project/pallas_call | solution.py:108
  4.6 0.5 %collective-permute-start = (f32[10,64,128]{2,1,0:T(8,128)S(1)}, f32[10,64,128]{2,1,0:T(8,128)S(1)}, u32[]{:S(2)}, u32[]{:S(2)}) collective-permute-start(f32[10,64,128]{2,1,0:T(8,128)S(1)} %get-tuple-element.28), channel_id=1, source_target_pairs={{0,1},{1,0},{2,3},{3,2},{4,5},{5,4},{6,7},{7,6},{8,9},{9,8},{10,11... | collective-permute-start | bytes 983048 | tf_op jit(solution)/shard_map/ppermute | solution.py:231
  5.2 0.1 collective-permute-start.4
  5.2 1.5 %project_kept.1.refs_0_.held.query = f32[10,64,128]{2,1,0:T(8,128)S(1)} custom-call(bf16[8,1,128,1792]{3,2,1,0:T(8,128)(2,1)S(1)} %get-tuple-element.29.train, bf16[2,128,1792]{2,1,0:T(8,128)(2,1)S(1)} %get-tuple-element.30.query, bf16[64,1792]{1,0:T(8,128)(2,1)S(1)} %get-tuple-element.31.proj), custom_call_target="tpu_custom_call" | custom-call | flops 293601280 | bytes 4587520 | tf_op jit(solution)/shard_map/project_kept/pallas_call | solution.py:140
  6.7 0.0 collective-permute-done.got
  6.8 3.1 %collective-permute-start.1 = (f32[6,64,128]{2,1,0:T(8,128)S(1)}, f32[6,64,128]{2,1,0:T(8,128)S(1)}, u32[]{:S(2)}, u32[]{:S(2)}) collective-permute-start(f32[6,64,128]{2,1,0:T(8,128)S(1)} %get-tuple-element.33.query), channel_id=1, source_target_pairs={{0,4},{1,3},{2,6},{3,1},{4,0},{5,7},{6,2},{7,5},{8,12},{9,11},{10,... | collective-permute-start | bytes 589832 | tf_op jit(solution)/shard_map/ppermute | solution.py:231
  9.9 0.0 collective-permute-done.4.got
  9.9 0.1 collective-permute-start.5
  10.0 3.5 %collective-permute-done.1.got = f32[6,64,128]{2,1,0:T(8,128)S(1)} collective-permute-done((f32[6,64,128]{2,1,0:T(8,128)S(1)}, f32[6,64,128]{2,1,0:T(8,128)S(1)}, u32[]{:S(2)}, u32[]{:S(2)}) %collective-permute-start.1) | collective-permute-done | bytes 196640 | tf_op jit(solution)/shard_map/ppermute | solution.py:231
  13.6 2.0 %collective-permute-start.2 = (f32[4,64,128]{2,1,0:T(8,128)S(1)}, f32[4,64,128]{2,1,0:T(8,128)S(1)}, u32[]{:S(2)}, u32[]{:S(2)}) collective-permute-start(f32[4,64,128]{2,1,0:T(8,128)S(1)} %get-tuple-element.35.query), channel_id=1, source_target_pairs={{0,2},{1,9},{2,0},{3,11},{4,6},{5,13},{6,4},{7,15},{8,10},{9,1},{1... | collective-permute-start | bytes 393224 | tf_op jit(solution)/shard_map/ppermute | solution.py:231
  15.6 0.1 collective-permute-done.5.got
  15.7 2.0 %collective-permute-start.6 = (f32[4,64,128]{2,1,0:T(8,128)S(1)}, f32[4,64,128]{2,1,0:T(8,128)S(1)}, u32[]{:S(2)}, u32[]{:S(2)}) collective-permute-start(f32[4,64,128]{2,1,0:T(8,128)S(1)} %get-tuple-element.43.query), channel_id=1, source_target_pairs={{0,2},{1,9},{2,0},{3,11},{4,6},{5,13},{6,4},{7,15},{8,10},{9,1},{1... | collective-permute-start | bytes 393224 | tf_op jit(solution)/shard_map/ppermute | solution.py:231
  17.7 0.9 %collective-permute-done.2.got = f32[4,64,128]{2,1,0:T(8,128)S(1)} collective-permute-done((f32[4,64,128]{2,1,0:T(8,128)S(1)}, f32[4,64,128]{2,1,0:T(8,128)S(1)}, u32[]{:S(2)}, u32[]{:S(2)}) %collective-permute-start.2) | collective-permute-done | bytes 131104 | tf_op jit(solution)/shard_map/ppermute | solution.py:231
  18.6 3.1 %collective-permute-start.3 = (f32[3,64,128]{2,1,0:T(8,128)S(1)}, f32[3,64,128]{2,1,0:T(8,128)S(1)}, u32[]{:S(2)}, u32[]{:S(2)}) collective-permute-start(f32[3,64,128]{2,1,0:T(8,128)S(1)} %get-tuple-element.37.query), channel_id=1, source_target_pairs={{0,8},{1,5},{2,10},{3,7},{4,12},{5,1},{6,14},{7,3},{8,0},{9,13},{1... | collective-permute-start | bytes 294920 | tf_op jit(solution)/shard_map/ppermute | solution.py:231
  21.7 0.0 collective-permute-done.6.got
  21.7 2.3 %collective-permute-start.7 = (f32[3,64,128]{2,1,0:T(8,128)S(1)}, f32[3,64,128]{2,1,0:T(8,128)S(1)}, u32[]{:S(2)}, u32[]{:S(2)}) collective-permute-start(f32[3,64,128]{2,1,0:T(8,128)S(1)} %get-tuple-element.45.query), channel_id=1, source_target_pairs={{0,8},{1,5},{2,10},{3,7},{4,12},{5,1},{6,14},{7,3},{8,0},{9,13},{1... | collective-permute-start | bytes 294920 | tf_op jit(solution)/shard_map/ppermute | solution.py:231
  24.1 0.8 %collective-permute-done.3.got = f32[3,64,128]{2,1,0:T(8,128)S(1)} collective-permute-done((f32[3,64,128]{2,1,0:T(8,128)S(1)}, f32[3,64,128]{2,1,0:T(8,128)S(1)}, u32[]{:S(2)}, u32[]{:S(2)}) %collective-permute-start.3) | collective-permute-done | bytes 98336 | tf_op jit(solution)/shard_map/ppermute | solution.py:231
  24.9 0.1 collective-permute-start.8
  24.9 2.4 %collective-permute-done.7.got = f32[3,64,128]{2,1,0:T(8,128)S(1)} collective-permute-done((f32[3,64,128]{2,1,0:T(8,128)S(1)}, f32[3,64,128]{2,1,0:T(8,128)S(1)}, u32[]{:S(2)}, u32[]{:S(2)}) %collective-permute-start.7) | collective-permute-done | bytes 98336 | tf_op jit(solution)/shard_map/ppermute | solution.py:231
  27.3 0.1 collective-permute-start.9
  27.4 0.0 collective-permute-done.8.other_a
  27.4 1.2 %collective-permute-done.9.other_b = bf16[2,64,128]{2,1,0:T(8,128)(2,1)S(1)} collective-permute-done((bf16[2,64,128]{2,1,0:T(8,128)(2,1)S(1)}, bf16[2,64,128]{2,1,0:T(8,128)(2,1)S(1)}, u32[]{:S(2)}, u32[]{:S(2)}) %collective-permute-start.9) | collective-permute-done | bytes 32800 | tf_op jit(solution)/shard_map/ppermute | solution.py:231
  28.6 0.8 %score.1 = f32[1,4]{1,0:T(1,128)} custom-call(bf16[1,64,128]{2,1,0:T(8,128)(2,1)S(1)} %get-tuple-element.38.own_a, bf16[1,64,128]{2,1,0:T(8,128)(2,1)S(1)} %get-tuple-element.46.own_b, bf16[2,64,128]{2,1,0:T(8,128)(2,1)S(1)} %get-tuple-element.47.mine_a, bf16[2,64,128]{2,1,0:T(8,128)(2,1)S(1)} %get-tuple-element.48.mine_b, ...), custom_call_target="tpu_custom_call" | custom-call | tf_op jit(solution)/shard_map/score/pallas_call | solution.py:218
  (8 shorter events, 0.2 us)
Async XLA Ops:
  4.6 2.1 %collective-permute-start = (f32[10,64,128]{2,1,0:T(8,128)S(1)}, f32[10,64,128]{2,1,0:T(8,128)S(1)}, u32[]{:S(2)}, u32[]{:S(2)}) collective-permute-start(f32[10,64,128]{2,1,0:T(8,128)S(1)} %get-tuple-element.28), channel_id=1, source_target_pairs={{0,1},{1,0},{2,3},{3,2},{4,5},{5,4},{6,7},{7,6},{8,9},{9,8},{10,11... | collective-permute-start | bytes 983048 | tf_op jit(solution)/shard_map/ppermute | solution.py:231
  5.2 4.7 %collective-permute-start.4 = (f32[10,64,128]{2,1,0:T(8,128)S(1)}, f32[10,64,128]{2,1,0:T(8,128)S(1)}, u32[]{:S(2)}, u32[]{:S(2)}) collective-permute-start(f32[10,64,128]{2,1,0:T(8,128)S(1)} %get-tuple-element.39), channel_id=1, source_target_pairs={{0,1},{1,0},{2,3},{3,2},{4,5},{5,4},{6,7},{7,6},{8,9},{9,8},{10,11... | collective-permute-start | bytes 983048 | tf_op jit(solution)/shard_map/ppermute | solution.py:231
  6.8 6.7 %collective-permute-start.1 = (f32[6,64,128]{2,1,0:T(8,128)S(1)}, f32[6,64,128]{2,1,0:T(8,128)S(1)}, u32[]{:S(2)}, u32[]{:S(2)}) collective-permute-start(f32[6,64,128]{2,1,0:T(8,128)S(1)} %get-tuple-element.33.query), channel_id=1, source_target_pairs={{0,4},{1,3},{2,6},{3,1},{4,0},{5,7},{6,2},{7,5},{8,12},{9,11},{10,... | collective-permute-start | bytes 589832 | tf_op jit(solution)/shard_map/ppermute | solution.py:231
  9.9 5.7 %collective-permute-start.5 = (f32[6,64,128]{2,1,0:T(8,128)S(1)}, f32[6,64,128]{2,1,0:T(8,128)S(1)}, u32[]{:S(2)}, u32[]{:S(2)}) collective-permute-start(f32[6,64,128]{2,1,0:T(8,128)S(1)} %get-tuple-element.41.query), channel_id=1, source_target_pairs={{0,4},{1,3},{2,6},{3,1},{4,0},{5,7},{6,2},{7,5},{8,12},{9,11},{10,... | collective-permute-start | bytes 589832 | tf_op jit(solution)/shard_map/ppermute | solution.py:231
  13.6 5.0 %collective-permute-start.2 = (f32[4,64,128]{2,1,0:T(8,128)S(1)}, f32[4,64,128]{2,1,0:T(8,128)S(1)}, u32[]{:S(2)}, u32[]{:S(2)}) collective-permute-start(f32[4,64,128]{2,1,0:T(8,128)S(1)} %get-tuple-element.35.query), channel_id=1, source_target_pairs={{0,2},{1,9},{2,0},{3,11},{4,6},{5,13},{6,4},{7,15},{8,10},{9,1},{1... | collective-permute-start | bytes 393224 | tf_op jit(solution)/shard_map/ppermute | solution.py:231
  15.7 6.0 %collective-permute-start.6 = (f32[4,64,128]{2,1,0:T(8,128)S(1)}, f32[4,64,128]{2,1,0:T(8,128)S(1)}, u32[]{:S(2)}, u32[]{:S(2)}) collective-permute-start(f32[4,64,128]{2,1,0:T(8,128)S(1)} %get-tuple-element.43.query), channel_id=1, source_target_pairs={{0,2},{1,9},{2,0},{3,11},{4,6},{5,13},{6,4},{7,15},{8,10},{9,1},{1... | collective-permute-start | bytes 393224 | tf_op jit(solution)/shard_map/ppermute | solution.py:231
  18.6 6.2 %collective-permute-start.3 = (f32[3,64,128]{2,1,0:T(8,128)S(1)}, f32[3,64,128]{2,1,0:T(8,128)S(1)}, u32[]{:S(2)}, u32[]{:S(2)}) collective-permute-start(f32[3,64,128]{2,1,0:T(8,128)S(1)} %get-tuple-element.37.query), channel_id=1, source_target_pairs={{0,8},{1,5},{2,10},{3,7},{4,12},{5,1},{6,14},{7,3},{8,0},{9,13},{1... | collective-permute-start | bytes 294920 | tf_op jit(solution)/shard_map/ppermute | solution.py:231
  21.7 5.6 %collective-permute-start.7 = (f32[3,64,128]{2,1,0:T(8,128)S(1)}, f32[3,64,128]{2,1,0:T(8,128)S(1)}, u32[]{:S(2)}, u32[]{:S(2)}) collective-permute-start(f32[3,64,128]{2,1,0:T(8,128)S(1)} %get-tuple-element.45.query), channel_id=1, source_target_pairs={{0,8},{1,5},{2,10},{3,7},{4,12},{5,1},{6,14},{7,3},{8,0},{9,13},{1... | collective-permute-start | bytes 294920 | tf_op jit(solution)/shard_map/ppermute | solution.py:231
  24.9 2.6 %collective-permute-start.8 = (bf16[2,64,128]{2,1,0:T(8,128)(2,1)S(1)}, bf16[2,64,128]{2,1,0:T(8,128)(2,1)S(1)}, u32[]{:S(2)}, u32[]{:S(2)}) collective-permute-start(bf16[2,64,128]{2,1,0:T(8,128)(2,1)S(1)} %get-tuple-element.47.mine_a), channel_id=1, source_target_pairs={{0,1},{1,0},{2,3},{3,2},{4,5},{5,4},{6,7},{7,6},{8,9},{9,8},{10,11... | collective-permute-start | bytes 98312 | tf_op jit(solution)/shard_map/ppermute | solution.py:231
  27.3 1.3 %collective-permute-start.9 = (bf16[2,64,128]{2,1,0:T(8,128)(2,1)S(1)}, bf16[2,64,128]{2,1,0:T(8,128)(2,1)S(1)}, u32[]{:S(2)}, u32[]{:S(2)}) collective-permute-start(bf16[2,64,128]{2,1,0:T(8,128)(2,1)S(1)} %get-tuple-element.48.mine_b), channel_id=1, source_target_pairs={{0,1},{1,0},{2,3},{3,2},{4,5},{5,4},{6,7},{7,6},{8,9},{9,8},{10,11... | collective-permute-start | bytes 98312 | tf_op jit(solution)/shard_map/ppermute | solution.py:231
